TPU v7x, 128 devices: a whole 4x4x4 slice. The times are simulated.
128 devices in a mesh: mem: 8 (over y, core), tile: 16 (over z, x).
Axes of the slice: x: 4, y: 4, z: 4, core: 2. Of those that a mesh axis runs over, the one named last changes fastest.
Arguments:
- noisy: bfloat16 [16, 128, 32, 256], P('mem', 'tile'), may hold values from -6 to 6
- timestep: int32 [16], P('mem'), may hold values from 500 to 999
- seams: int32 [128, 4, 3], P('tile'), may hold values from 0 to 127, as said below
- corner_list: int32 [128, 4, 2], P('tile'), may hold values from 0 to 127, as said below
- route: int32 [128, 1], replicated, may hold values from 0 to 15; in each aligned block of 8 rows (0 to 7, 8 to 15, ...) at most 2 rows name the same one
- target_block: int32 [128], replicated, may hold values from 0 to 3
- frac: float32 [128, 2], P('tile'), may hold values from 0.05 to 0.95
- w_time: float32 [128, 128], replicated, may hold values from -0.5 to 0.5
- w_lift: bfloat16 [8, 128], replicated, may hold values from -2 to 2
- w_fine: bfloat16 [9, 128, 128], replicated, may hold values from -0.1875 to 0.1875
- w_coarse: bfloat16 [9, 128, 128], replicated, may hold values from -0.1875 to 0.1875
- gain_fine: float32 [128], replicated, may hold values from 0.1 to 1.9
- gain_coarse: float32 [128], replicated, may hold values from 0.1 to 1.9
- gain_out: float32 [128], replicated, may hold values from 0.1 to 1.9
- w_out: bfloat16 [128, 8], replicated, may hold values from -0.5 to 0.5
Outputs:
- denoised: float32 [16, 128, 32, 256], P('mem', 'tile')
- ens_mean: float32 [64, 32, 256], P('tile')
- ens_spread: float32 [64, 32, 256], P('tile')
Inputs may be any that keep to these rules, and one draw needn't show every extreme that they name: seams[t,k] = (neighbour sub-tile, its touching side 0..3, reversal flag 0 or 1), with sub-tiles numbered 8 to an index of tile in order. Every side is paired with exactly one side, symmetrically and with the same reversal flag at both ends: the east side of a sub-tile touches the west side of a sub-tile on the next index of tile (cyclically), and the north side touches the south side of a sub-tile on the same index. corner_list[t,k] = (sub-tile, its corner 0..3), following from seams: corners 0 and 1 are corners 3 and 2 of the north neighbour, corners 2 and 3 are corners 1 and 0 of the south neighbour, each pair swapped where that seam is reversed. `route`: of the sub-tiles of one index of tile, at most 2 go to one owner, and some index sends exactly 2 to some owner.
All inputs are finite; a program needn't handle non-finite values.
Results may differ from a plain program's by a relative error of at most 0.01.
Values may be sent and summed in bfloat16 or wider, within the bound.
A program may use at most 128 MiB of HBM per device.

v0:
```python
import math

import jax
import jax.numpy as jnp
from jax import lax
from jax.sharding import PartitionSpec as P

STEPS = 1000


def with_halo(cells, sides, width):
    for axis, dim in sides:
        count = lax.axis_size(axis)
        head = lax.slice_in_dim(cells, 0, width, axis=dim)
        tail = lax.slice_in_dim(cells, cells.shape[dim] - width, cells.shape[dim], axis=dim)
        cells = jnp.concatenate(
            [
                lax.ppermute(tail, axis, [(i, (i + 1) % count) for i in range(count)]),
                cells,
                lax.ppermute(head, axis, [((i + 1) % count, i) for i in range(count)]),
            ],
            axis=dim,
        )
    return cells


def precondition(timestep):
    fraction = timestep.astype(jnp.float32) / (STEPS - 1)
    high_root = 80.0 ** (1.0 / 7.0)
    low_root = 0.002 ** (1.0 / 7.0)
    sigma = (high_root + fraction * (low_root - high_root)) ** 7
    denominator = sigma * sigma + 1.0
    return (lax.rsqrt(denominator), 1.0 / denominator, sigma * lax.rsqrt(denominator))


def embed(timestep, w_time):
    half_width = w_time.shape[0] // 2
    frequency = jnp.exp(-math.log(10000.0) * jnp.arange(half_width, dtype=jnp.float32) / half_width)
    angles = timestep.astype(jnp.float32)[:, None] * frequency[None, :]
    features = jnp.concatenate([jnp.sin(angles), jnp.cos(angles)], axis=-1)
    return jax.nn.silu(jnp.dot(features, w_time, precision=lax.Precision.HIGHEST))


def rms_act(activation, gain):
    values = activation.astype(jnp.float32)
    normed = values * lax.rsqrt(jnp.mean(values * values, axis=-1, keepdims=True) + 1e-06) * gain
    return jax.nn.silu(normed).astype(jnp.bfloat16)


def rims_of(normed):
    edge_len = normed.shape[2]
    north_rim = normed[:, :, 0]
    east_rim = normed[:, :, :, edge_len - 1]
    south_rim = normed[:, :, edge_len - 1]
    west_rim = normed[:, :, :, 0]
    corners = jnp.stack(
        [
            normed[:, :, 0, 0],
            normed[:, :, 0, edge_len - 1],
            normed[:, :, edge_len - 1, edge_len - 1],
            normed[:, :, edge_len - 1, 0],
        ],
        axis=2,
    )
    return jnp.concatenate([north_rim, east_rim, south_rim, west_rim, corners], axis=2)


def halo_rows(tile_refs, corner_refs, seams, corner_list, edge_len):
    width = 4 * edge_len + 4
    positions = jnp.arange(edge_len, dtype=jnp.int32)
    along_edge = jnp.where(
        seams[:, :, 2:3] == 1, edge_len - 1 - positions[None, None, :], positions[None, None, :]
    )
    edge_rows = tile_refs[:, :, None] * width + seams[:, :, 1:2] * edge_len + along_edge
    corner_rows = corner_refs * width + 4 * edge_len + corner_list[:, :, 1]
    edge_rows = edge_rows.reshape(edge_rows.shape[0], 4 * edge_len)
    return jnp.concatenate([edge_rows, corner_rows], axis=1)


def assemble(normed, gathered):
    edge_len = normed.shape[2]
    north_rim = gathered[:, :, 0:edge_len]
    east_rim = gathered[:, :, edge_len : 2 * edge_len]
    south_rim = gathered[:, :, 2 * edge_len : 3 * edge_len]
    west_rim = gathered[:, :, 3 * edge_len : 4 * edge_len]
    corners = gathered[:, :, 4 * edge_len :]
    middle = jnp.concatenate([west_rim[:, :, :, None], normed, east_rim[:, :, :, None]], axis=3)
    upper_row = jnp.concatenate([corners[:, :, 0:1], north_rim, corners[:, :, 1:2]], axis=2)[
        :, :, None
    ]
    lower_row = jnp.concatenate([corners[:, :, 3:4], south_rim, corners[:, :, 2:3]], axis=2)[
        :, :, None
    ]
    return jnp.concatenate([upper_row, middle, lower_row], axis=2)


def convolve(padded, weight):
    members, tile_total, edge_len = (padded.shape[0], padded.shape[1], padded.shape[2] - 2)
    channels = padded.shape[-1]
    summed = jnp.zeros((members * tile_total * edge_len * edge_len, weight.shape[2]), jnp.float32)
    for row_off in range(3):
        for col_off in range(3):
            slab_view = padded[
                :, :, row_off : row_off + edge_len, col_off : col_off + edge_len
            ].reshape(-1, channels)
            summed = summed + jnp.dot(
                slab_view, weight[3 * row_off + col_off], preferred_element_type=jnp.float32
            )
    return summed.reshape(members, tile_total, edge_len, edge_len, weight.shape[2])


def level_step(activation, gain, weight, rows, window_fn):
    normed = rms_act(activation, gain)
    window = window_fn(rims_of(normed))
    members, tile_total = (normed.shape[0], normed.shape[1])
    flattened = window.reshape(members, -1, window.shape[-1])
    gathered = jnp.take(flattened, rows.reshape(-1), axis=1).reshape(
        members, tile_total, rows.shape[1], window.shape[-1]
    )
    padded = assemble(normed, gathered)
    return (activation.astype(jnp.float32) + convolve(padded, weight)).astype(jnp.bfloat16)


def denoise(noisy, timestep, fine_rows, coarse_rows, weights, fine_fn, coarse_fn):
    w_time, w_lift, w_fine, w_coarse, gain_fine, gain_coarse, gain_out, w_out = weights
    members, tile_total, edge_len, packed = noisy.shape
    variables = packed // edge_len
    channels = w_lift.shape[1]
    scale_in, scale_skip, scale_out = precondition(timestep)
    temb = embed(timestep, w_time)
    scaled = (noisy.astype(jnp.float32) * scale_in[:, None, None, None]).astype(jnp.bfloat16)
    lifted = jnp.dot(scaled.reshape(-1, variables), w_lift, preferred_element_type=jnp.float32)
    lifted = lifted.reshape(members, tile_total, edge_len, edge_len, channels)
    started = (lifted + temb[:, None, None, None, :]).astype(jnp.bfloat16)
    fine_out = level_step(started, gain_fine, w_fine, fine_rows, fine_fn)
    half_len = edge_len // 2
    pooled = fine_out.astype(jnp.float32).reshape(
        members, tile_total, half_len, 2, half_len, 2, channels
    )
    pooled = (jnp.sum(pooled, axis=(3, 5)) * 0.25).astype(jnp.bfloat16)
    coarse = level_step(pooled, gain_coarse, w_coarse, coarse_rows, coarse_fn)
    upsampled = jnp.repeat(
        jnp.repeat(coarse.astype(jnp.float32), 2, axis=2), 2, axis=3
    ) + fine_out.astype(jnp.float32)
    final_act = rms_act(upsampled, gain_out)
    projected = jnp.dot(final_act.reshape(-1, channels), w_out, preferred_element_type=jnp.float32)
    projected = projected.reshape(members, tile_total, edge_len, packed)
    result = (
        scale_skip[:, None, None, None] * noisy.astype(jnp.float32)
        + scale_out[:, None, None, None] * projected
    )
    return result


def remap(denoised, frac, variables):
    frac_rows = frac[:, 0][None, :, None, None]
    frac_cols = frac[:, 1][None, :, None, None]
    rows_next = jnp.concatenate([denoised[:, :, 1:], denoised[:, :, -1:]], axis=2)
    row_mixed = (1.0 - frac_rows) * denoised + frac_rows * rows_next
    cols_next = jnp.concatenate([row_mixed[..., variables:], row_mixed[..., -variables:]], axis=3)
    return (1.0 - frac_cols) * row_mixed + frac_cols * cols_next


def on_device(
    noisy,
    timestep,
    seams,
    corner_list,
    route,
    target_block,
    frac,
    w_time,
    w_lift,
    w_fine,
    w_coarse,
    gain_fine,
    gain_coarse,
    gain_out,
    w_out,
):
    members, tiles_here, edge_len, packed = noisy.shape
    variables = packed // edge_len
    position = lax.axis_index("tile")
    tile_count = lax.axis_size("tile")

    def window_ids(tile_refs):
        return (
            tile_refs // tiles_here - position + 1
        ) % tile_count * tiles_here + tile_refs % tiles_here

    tile_refs = window_ids(seams[:, :, 0])
    corner_refs = window_ids(corner_list[:, :, 0])
    fine_rows = halo_rows(tile_refs, corner_refs, seams, corner_list, edge_len)
    coarse_rows = halo_rows(tile_refs, corner_refs, seams, corner_list, edge_len // 2)

    def fine_fn(rim_cells):
        window = with_halo(rim_cells, (("tile", 1),), tiles_here)
        return window

    def coarse_fn(rim_cells):
        window = with_halo(rim_cells, (("tile", 1),), tiles_here)
        return window

    weights = (w_time, w_lift, w_fine, w_coarse, gain_fine, gain_coarse, gain_out, w_out)
    denoised = denoise(noisy, timestep, fine_rows, coarse_rows, weights, fine_fn, coarse_fn)
    remapped = remap(denoised, frac, variables)
    flattened = remapped.reshape(members, tiles_here, edge_len * packed)
    block_here = tiles_here // 2
    owners = route[:, 0]
    own_owner = lax.dynamic_slice_in_dim(owners, position * tiles_here, tiles_here)
    own_block = lax.dynamic_slice_in_dim(target_block, position * tiles_here, tiles_here)
    global_block = own_owner * block_here + own_block
    selector = (
        jnp.arange(tile_count * block_here, dtype=jnp.int32)[:, None] == global_block[None, :]
    ).astype(jnp.float32)
    dense = jnp.einsum("bt,mtx->mbx", selector, flattened, precision=lax.Precision.HIGHEST)
    target = lax.psum_scatter(dense, "tile", scatter_dimension=1, tiled=True)
    total_members = members * lax.axis_size("mem")
    summed = lax.psum(jnp.sum(target, axis=0), "mem")
    ens_mean = summed / total_members
    deviation = target - ens_mean[None]
    squares = lax.psum(jnp.sum(deviation * deviation, axis=0), "mem")
    ens_spread = jnp.sqrt(squares / (total_members - 1) + 1e-06)
    ens_mean = ens_mean.reshape(block_here, edge_len, packed)
    ens_spread = ens_spread.reshape(block_here, edge_len, packed)
    return (denoised, ens_mean, ens_spread)


def solution(mesh):
    placed = (
        P("mem", "tile", None, None),
        P("mem"),
        P("tile", None, None),
        P("tile", None, None),
        P(),
        P(),
        P("tile", None),
        P(),
        P(),
        P(),
        P(),
        P(),
        P(),
        P(),
        P(),
    )
    return jax.shard_map(
        on_device,
        mesh=mesh,
        in_specs=placed,
        out_specs=(P("mem", "tile", None, None), P("tile", None, None), P("tile", None, None)),
        check_vma=False,
    )
```

profile of v0, /device:TPU:1, one launch (start us, length us, event | category | flops | bytes accessed | tf_op | source)
XLA Modules:
  0.0 427.7 jit_solution(11695723547498630574)
XLA Ops:
  12.8 3.6 fusion
  24.2 5.0 %collective-permute-start.1 = (bf16[2,8,132,128]{3,1,2,0:T(8,128)(2,1)S(1)}, bf16[2,8,132,128]{3,1,2,0:T(8,128)(2,1)S(1)}, u32[]{:S(2)}, u32[]{:S(2)}) collective-permute-start(bf16[2,8,132,128]{3,1,2,0:T(8,128)(2,1)S(1)} %copy.188), channel_id=1, source_target_pairs={{1,0},{2,1},{3,2},{4,3},{5,4},{6,5},{7,6},{8,7},{9,8},{10,9},{11,1... | collective-permute-start | bytes 1622024 | tf_op jit(solution)/shard_map/ppermute | solution.py:20
  31.7 9.2 %collective-permute-done = bf16[2,8,132,128]{3,1,2,0:T(8,128)(2,1)S(1)} collective-permute-done((bf16[2,8,132,128]{3,1,2,0:T(8,128)(2,1)S(1)}, bf16[2,8,132,128]{3,1,2,0:T(8,128)(2,1)S(1)}, u32[]{:S(2)}, u32[]{:S(2)}) %collective-permute-start) | collective-permute-done | bytes 540704 | tf_op jit(solution)/shard_map/ppermute | solution.py:18
  43.0 4.3 %gather_fusion = bf16[1056,2,128]{2,1,0:T(2,128)(2,1)S(1)} fusion(bf16[2,3168,128]{2,0,1:T(2,128)(2,1)S(1)} %bitcast.238, s32[2048]{0:T(1024)S(1)} %pad_clamp_fusion), kind=kCustom, calls=%fused_computation | custom fusion | bytes 1085568 | tf_op jit(solution)/shard_map/jit(_take)/gather | solution.py:117
  48.1 9.4 %pad_maximum_fusion.1 = (bf16[2,8,32,32,128]{4,3,2,1,0:T(8,128)(2,1)S(1)}, bf16[2,8,32,32,128]{4,3,2,1,0:T(8,128)(2,1)}) fusion(bf16[2,8,32,1,128]{4,3,2,1,0:T(2,128)(2,1)S(1)} %copy.195, bf16[2,8,32,32,128]{4,3,2,1,0:T(8,128)(2,1)} %copy-done.2, bf16[2,8,32,1,128]{4,3,2,1,0:T(2,128)(2,1)S(1)} %copy.194), kind=kLoop, calls=%fused_computation.37 | loop fusion | flops 16777216 | bytes 12845056 | tf_op jit(solution)/shard_map/concatenate | solution.py:87
  57.7 6.1 %pad_maximum_fusion = (bf16[2,8,33,34,128]{4,3,2,1,0:T(8,128)(2,1)S(1)}, bf16[2,8,33,34,128]{4,3,2,1,0:T(8,128)(2,1)S(1)}) fusion(bf16[2,8,1,34,128]{4,3,2,1,0:T(8,128)(2,1)S(1)} %get-tuple-element.90, bf16[2,8,32,1,128]{4,3,2,1,0:T(2,128)(2,1)S(1)} %copy.195, bf16[2,8,32,32,128]{4,3,2,1,0:T(8,128)(2,1)S(1)} %copy-done.3, ...), kind=kLoop, calls=%fused_computation.27 | loop fusion | flops 36765696 | bytes 13926400 | tf_op jit(solution)/shard_map/concatenate | solution.py:94
  63.8 5.0 %fusion.96 = (bf16[2,8,32,32,128]{4,3,2,1,0:T(8,128)(2,1)S(1)}, bf16[2,8,32,32,128]{4,3,2,1,0:T(8,128)(2,1)}, bf16[2,8,32,32,128]{4,3,2,1,0:T(8,128)(2,1)}) fusion(bf16[2,8,33,34,128]{4,3,2,1,0:T(8,128)(2,1)S(1)} %get-tuple-element.32), kind=kLoop, calls=%fused_computation.219 | loop fusion | bytes 25165824 | tf_op jit(solution)/shard_map/slice | solution.py:103
  68.7 7.1 %fusion.95 = (bf16[2,8,32,32,128]{4,3,2,1,0:T(8,128)(2,1)}, bf16[2,8,32,32,128]{4,3,2,1,0:T(8,128)(2,1)}, bf16[2,8,32,32,128]{4,3,2,1,0:T(8,128)(2,1)}) fusion(bf16[2,8,33,34,128]{4,3,2,1,0:T(8,128)(2,1)S(1)} %get-tuple-element.31), kind=kLoop, calls=%fused_computation.218 | loop fusion | bytes 25165824 | tf_op jit(solution)/shard_map/slice | solution.py:103
  75.9 3.4 fusion.43
  84.0 3.4 convolution_add_fusion.5
  89.9 3.6 convolution_add_fusion.2
  97.8 5.3 %fusion.9 = f32[2,8,32,32,128]{4,3,2,1,0:T(8,128)} fusion(f32[2,8,32,32,128]{4,3,2,1,0:T(8,128)S(1)} %bitcast.216, bf16[2,8,32,32,128]{4,3,2,1,0:T(8,128)(2,1)S(1)} %copy-done.7), kind=kLoop, calls=%fused_computation.36 | loop fusion | flops 8388608 | bytes 20971520 | tf_op jit(solution)/shard_map/convert_element_type | solution.py:137
  103.1 9.6 %reduce_sum.55 = f32[2,8,16,16,128]{4,3,2,1,0:T(8,128)S(1)} reduce(f32[2,8,16,2,16,2,128]{6,5,4,3,2,1,0:T(2,128)} %bitcast.215, f32[]{:T(128)} %constant.143.clone.1), dimensions={3,5}, to_apply=%region_1.2 | reduce | flops 1572864 | bytes 10485764 | tf_op jit(solution)/shard_map/reduce_sum | solution.py:140
  118.5 4.8 %collective-permute-start.3 = (bf16[2,8,68,128]{3,2,1,0:T(8,128)(2,1)S(1)}, bf16[2,8,68,128]{3,2,1,0:T(8,128)(2,1)S(1)}, u32[]{:S(2)}, u32[]{:S(2)}) collective-permute-start(bf16[2,8,68,128]{3,2,1,0:T(8,128)(2,1)S(1)} %concatenate.91), channel_id=1, source_target_pairs={{1,0},{2,1},{3,2},{4,3},{5,4},{6,5},{7,6},{8,7},{9,8},{10,9},{11,1... | collective-permute-start | bytes 835592 | tf_op jit(solution)/shard_map/ppermute | solution.py:20
  124.0 5.1 %collective-permute-done.2 = bf16[2,8,68,128]{3,2,1,0:T(8,128)(2,1)S(1)} collective-permute-done((bf16[2,8,68,128]{3,2,1,0:T(8,128)(2,1)S(1)}, bf16[2,8,68,128]{3,2,1,0:T(8,128)(2,1)S(1)}, u32[]{:S(2)}, u32[]{:S(2)}) %collective-permute-start.2) | collective-permute-done | bytes 278560 | tf_op jit(solution)/shard_map/ppermute | solution.py:18
  143.6 5.7 %broadcast_in_dim.171 = f32[2,8,32,16,2,128]{5,4,3,2,1,0:T(2,128)} broadcast(f32[2,8,32,16,128]{4,3,2,1,0:T(8,128)S(1)} %bitcast.228), dimensions={0,1,2,3,5} | broadcast | bytes 12582912 | tf_op jit(solution)/shard_map/broadcast_in_dim | solution.py:142
  149.3 11.2 %multiply_reduce_fusion = (f32[2,8,32,32]{3,2,1,0:T(8,128)S(1)}, f32[2,8,32,32,128]{4,3,2,1,0:T(8,128)}) fusion(f32[2,8,32,32,128]{4,3,2,1,0:T(8,128)} %bitcast.217, f32[2,8,32,32,128]{4,3,2,1,0:T(8,128)} %fusion.9), kind=kLoop, calls=%fused_computation.24 | loop fusion | flops 6275072 | bytes 25231360 | tf_op jit(solution)/shard_map/reduce_sum | solution.py:46
  160.5 5.3 %multiply_convert_fusion = bf16[2,8,32,32,128]{4,3,2,1,0:T(8,128)(2,1)S(1)} fusion(f32[2,8,32,32,128]{4,3,2,1,0:T(8,128)} %get-tuple-element.18, f32[128]{0:T(128)S(1)} %copy-done.19, f32[2,8,32,32]{3,2,1,0:T(8,128)S(1)} %add_rsqrt_fusion), kind=kLoop, calls=%fused_computation.23 | loop fusion | flops 14680064 | bytes 12648960 | tf_op jit(solution)/shard_map/convert_element_type | solution.py:47
  165.9 4.5 %fusion.106 = f32[16384,8]{1,0:T(8,128)} fusion(bf16[16384,128]{1,0:T(8,128)(2,1)S(1)} %bitcast.227, bf16[128,8]{0,1:T(8,128)(2,1)S(1)} %copy-done.17), kind=kOutput, calls=%fused_computation.229 | convolution fusion | flops 33554432 | bytes 4720640 | tf_op jit(solution)/shard_map/dot_general | solution.py:146
  170.4 7.2 %reshape.334 = f32[2,8,32,256]{3,2,1,0:T(8,128)S(1)} reshape(f32[16384,8]{1,0:T(8,128)} %fusion.106) | data formatting | bytes 1048576 | tf_op jit(solution)/shard_map/reshape | solution.py:147
  188.1 3.9 convolution_bitcast_fusion
  193.3 104.6 %all-reduce.9.cloned.1.call-done = f32[2,64,8192]{2,1,0:T(8,128)} async-done(((f32[2,64,8192]{2,1,0:T(8,128)}), f32[2,64,8192]{2,1,0:T(8,128)}) %all-reduce.9.cloned.1.call-update) | async-done | bytes 4194320
  299.8 58.0 %all-reduce.5.cloned.1.call-done = f32[4,8192]{1,0:T(4,128)} async-done(((f32[4,8192]{1,0:T(4,128)}), f32[4,8192]{1,0:T(4,128)}) %all-reduce.5.cloned.1.call-update) | async-done | bytes 131088 | tf_op jit(solution)/shard_map/psum | solution.py:219
  362.7 56.5 %all-reduce.7.cloned.1.call-done = f32[4,8192]{1,0:T(4,128)} async-done(((f32[4,8192]{1,0:T(4,128)}), f32[4,8192]{1,0:T(4,128)}) %all-reduce.7.cloned.1.call-update) | async-done | bytes 131088 | tf_op jit(solution)/shard_map/psum | solution.py:222
  (192 shorter events, 70.4 us)
Async XLA Ops:
  7.2 5.4 %copy-start = (f32[128,128]{1,0:T(8,128)S(1)}, f32[128,128]{1,0:T(8,128)}, u32[]{:S(2)}) copy-start(f32[128,128]{1,0:T(8,128)} %param.22) | copy-start | bytes 196612
  7.2 5.6 %copy-start.24 = (bf16[8,128]{1,0:T(8,128)(2,1)S(1)}, bf16[8,128]{1,0:T(8,128)(2,1)}, u32[]{:S(2)}) copy-start(bf16[8,128]{1,0:T(8,128)(2,1)} %param.23) | copy-start | bytes 6148
  7.2 290.7 %all-reduce.9.cloned.1.call-start = ((), (), s32[]{:S(2)}) async-start(), calls=%async_computation.2 | async-start | bytes 8388608
  11.1 5.3 %copy-start.8 = (bf16[2,8,32,256]{2,3,1,0:T(8,128)(2,1)}, bf16[2,8,32,256]{2,3,1,0:T(8,128)(2,1)S(1)}, u32[]{:S(2)}) copy-start(bf16[2,8,32,256]{2,3,1,0:T(8,128)(2,1)S(1)} %copy.177) | copy-start | bytes 786436
  19.8 9.5 %copy-start.13 = (s32[8,4,2]{0,2,1:T(2,128)S(1)}, s32[8,4,2]{0,2,1:T(2,128)}, u32[]{:S(2)}) copy-start(s32[8,4,2]{0,2,1:T(2,128)} %param.18) | copy-start | bytes 772
  19.8 9.5 %copy-start.12 = (s32[8,4,3]{0,1,2:T(4,128)S(1)}, s32[8,4,3]{0,1,2:T(4,128)}, u32[]{:S(2)}) copy-start(s32[8,4,3]{0,1,2:T(4,128)} %param.17) | copy-start | bytes 1156
  19.8 11.4 %copy-start.14 = (f32[8,2]{0,1:T(2,128)S(1)}, f32[8,2]{0,1:T(2,128)}, u32[]{:S(2)}) copy-start(f32[8,2]{0,1:T(2,128)} %param.21) | copy-start | bytes 196
  22.1 18.9 %collective-permute-start = (bf16[2,8,132,128]{3,1,2,0:T(8,128)(2,1)S(1)}, bf16[2,8,132,128]{3,1,2,0:T(8,128)(2,1)S(1)}, u32[]{:S(2)}, u32[]{:S(2)}) collective-permute-start(bf16[2,8,132,128]{3,1,2,0:T(8,128)(2,1)S(1)} %copy.188), channel_id=1, source_target_pairs={{0,1},{1,2},{2,3},{3,4},{4,5},{5,6},{6,7},{7,8},{8,9},{9,10},{10,1... | collective-permute-start | bytes 1622024 | tf_op jit(solution)/shard_map/ppermute | solution.py:18
  24.2 16.8 %collective-permute-start.1 = (bf16[2,8,132,128]{3,1,2,0:T(8,128)(2,1)S(1)}, bf16[2,8,132,128]{3,1,2,0:T(8,128)(2,1)S(1)}, u32[]{:S(2)}, u32[]{:S(2)}) collective-permute-start(bf16[2,8,132,128]{3,1,2,0:T(8,128)(2,1)S(1)} %copy.188), channel_id=1, source_target_pairs={{1,0},{2,1},{3,2},{4,3},{5,4},{6,5},{7,6},{8,7},{9,8},{10,9},{11,1... | collective-permute-start | bytes 1622024 | tf_op jit(solution)/shard_map/ppermute | solution.py:20
  48.1 9.5 %copy-start.3 = (bf16[2,8,32,32,128]{4,3,2,1,0:T(8,128)(2,1)S(1)}, bf16[2,8,32,32,128]{4,3,2,1,0:T(8,128)(2,1)}, u32[]{:S(2)}) copy-start(bf16[2,8,32,32,128]{4,3,2,1,0:T(8,128)(2,1)} %copy-done.2) | copy-start | bytes 12582916
  68.7 7.1 %copy-start.10 = (bf16[9,128,128]{2,1,0:T(8,128)(2,1)S(1)}, bf16[9,128,128]{2,1,0:T(8,128)(2,1)}, u32[]{:S(2)}) copy-start(bf16[9,128,128]{2,1,0:T(8,128)(2,1)} %param.24) | copy-start | bytes 884740
  103.1 10.3 %copy-start.23 = (f32[128]{0:T(128)S(1)}, f32[128]{0:T(128)}, u32[]{:S(2)}) copy-start(f32[128]{0:T(128)} %param.27) | copy-start | bytes 1540
  112.7 10.5 %copy-start.22 = (s32[128]{0:T(128)S(1)}, s32[128]{0:T(128)}, u32[]{:S(2)}) copy-start(s32[128]{0:T(128)} %param.20) | copy-start | bytes 1540
  118.4 10.7 %collective-permute-start.2 = (bf16[2,8,68,128]{3,2,1,0:T(8,128)(2,1)S(1)}, bf16[2,8,68,128]{3,2,1,0:T(8,128)(2,1)S(1)}, u32[]{:S(2)}, u32[]{:S(2)}) collective-permute-start(bf16[2,8,68,128]{3,2,1,0:T(8,128)(2,1)S(1)} %concatenate.91), channel_id=1, source_target_pairs={{0,1},{1,2},{2,3},{3,4},{4,5},{5,6},{6,7},{7,8},{8,9},{9,10},{10,1... | collective-permute-start | bytes 835592 | tf_op jit(solution)/shard_map/ppermute | solution.py:18
  118.5 10.6 %collective-permute-start.3 = (bf16[2,8,68,128]{3,2,1,0:T(8,128)(2,1)S(1)}, bf16[2,8,68,128]{3,2,1,0:T(8,128)(2,1)S(1)}, u32[]{:S(2)}, u32[]{:S(2)}) collective-permute-start(bf16[2,8,68,128]{3,2,1,0:T(8,128)(2,1)S(1)} %concatenate.91), channel_id=1, source_target_pairs={{1,0},{2,1},{3,2},{4,3},{5,4},{6,5},{7,6},{8,7},{9,8},{10,9},{11,1... | collective-permute-start | bytes 835592 | tf_op jit(solution)/shard_map/ppermute | solution.py:20
  149.3 11.2 %copy-start.19 = (f32[128]{0:T(128)S(1)}, f32[128]{0:T(128)}, u32[]{:S(2)}) copy-start(f32[128]{0:T(128)} %param.28) | copy-start | bytes 1540
  160.5 5.3 %copy-start.17 = (bf16[128,8]{0,1:T(8,128)(2,1)S(1)}, bf16[128,8]{0,1:T(8,128)(2,1)}, u32[]{:S(2)}) copy-start(bf16[128,8]{0,1:T(8,128)(2,1)} %param.29) | copy-start | bytes 6148
  170.4 9.2 %copy-start.9 = (bf16[2,8,32,256]{2,3,1,0:T(8,128)(2,1)S(1)}, bf16[2,8,32,256]{2,3,1,0:T(8,128)(2,1)}, u32[]{:S(2)}) copy-start(bf16[2,8,32,256]{2,3,1,0:T(8,128)(2,1)} %copy-done.8) | copy-start | bytes 786436
  170.4 9.2 %copy-start.20 = (f32[2]{0:T(128)S(1)}, f32[2]{0:T(128)}, u32[]{:S(2)}) copy-start(f32[2]{0:T(128)} %get-tuple-element.15) | copy-start | bytes 28
  170.4 9.2 %copy-start.21 = (f32[2]{0:T(128)S(1)}, f32[2]{0:T(128)}, u32[]{:S(2)}) copy-start(f32[2]{0:T(128)} %get-tuple-element.85) | copy-start | bytes 28
  188.1 4.0 copy-start.25
  192.0 228.9 %copy-start.1 = (f32[128,128]{1,0:T(8,128)S(1)}, f32[128,128]{1,0:T(8,128)}, u32[]{:S(2)}) copy-start(f32[128,128]{1,0:T(8,128)} %param.22) | copy-start | bytes 196612
  192.0 165.8 %all-reduce.5.cloned.1.call-start = ((), (), s32[]{:S(2)}) async-start(), calls=%async_computation | async-start | bytes 262144 | tf_op jit(solution)/shard_map/psum | solution.py:219
  299.8 119.5 %all-reduce.7.cloned.1.call-start = ((), (), s32[]{:S(2)}) async-start(), calls=%async_computation.1 | async-start | bytes 262144 | tf_op jit(solution)/shard_map/psum | solution.py:222
  (9 other events, 19.8 us)
Sparse Core Ops, SparseCore 0:
  192.1 105.7 all-reduce.8
  300.8 56.9 all-reduce.4
  360.9 58.3 all-reduce.6
where the time goes:
time: 434 us; the launch traced here: 428 us
  waiting for transfers between devices  233 us (54%)
  other arithmetic  70.3 us (16%)
  local copies, waits for them, and re-layouts  60.3 us (14%)
  matrix products  36 us (8%)
  between operations  15.5 us (4%)
  starting transfers between devices  12.1 us (3%)
    unnamed x4, waiting for transfers between devices  105 us
    psum x1, waiting for transfers between devices, on_device(): summed = lax.psum(jnp.sum(target, axis=0), 'mem')  58 us
    psum x1, waiting for transfers between devices, on_device(): squares = lax.psum(jnp.sum(deviation * deviation, axis=0), 'mem')  56.5 us
    dot_general x18, matrix products, convolve(): jnp.dot(slab_view, weight[3 * row_off + col_off], preferred_element_type=...  23.8 us
    ppermute x2, waiting for transfers between devices, with_halo(): lax.ppermute(tail, axis, [(i, (i + 1) % count) for i in range(count)])  14.3 us
    slice x4, local copies, waits for them, and re-layouts, convolve(): padded[:, :, row_off:row_off + edge_len, col_off:col_off + edge_len]  13.7 us
    reduce_sum x2, other arithmetic, rms_act(): jnp.mean(values * values, axis=-1, keepdims=True) + 1e-06  11.8 us
    concatenate x2, other arithmetic, assemble(): jnp.concatenate([west_rim[:, :, :, None], normed, east_rim[:, :, :, None]...  10.4 us
  transfers between devices with their start and end apart: 7, of which 5 were waited for; matrix products, arithmetic and copies ran while one was open for 1% of the time, Pallas kernels for 0%

commit v1 on v0

v1 whole, which is shorter than its diff:
```python
import functools
import math

import jax
import jax.numpy as jnp
from jax import lax
from jax.experimental import pallas as pl
from jax.experimental.pallas import tpu as pltpu
from jax.sharding import PartitionSpec as P

STEPS = 1000
MESH = pl.DeviceIdType.MESH
F32 = jnp.float32
BF16 = jnp.bfloat16

B = 16
N = 32
H = N // 2
NT = 16
NM = 8
CH = 4
RC = N // CH


def dot(a, b):
    return jnp.dot(a, b, preferred_element_type=F32)


def twice(x):
    return jnp.concatenate([x, x], axis=-1)


def iota(shape, dim):
    return lax.broadcasted_iota(jnp.int32, shape, dim)


def act(x, ones, half_gain):
    mean = dot((x * x).astype(BF16), ones)
    h = x * lax.rsqrt(mean + 1e-06) * half_gain
    return (h + h * jnp.tanh(h)).astype(BF16)


def seam_perm(perm_ref, seam_ref, side, n, natural):
    tile = seam_ref[:, 3 * side : 3 * side + 1] % 8
    flag = seam_ref[:, 3 * side + 2 : 3 * side + 3]
    base = (iota((B, 1), 0) // 8) * 8 + tile
    lane = iota((B, n * B), 1)

    def row(r, _):
        along = jnp.where(flag == 1, n - 1 - r, r)
        source = base * n + along if natural else along * B + base
        perm_ref[pl.ds(pl.multiple_of(r * B, B), B), :] = jnp.where(
            source == lane, 1.0, 0.0
        ).astype(BF16)
        return 0

    lax.fori_loop(0, n, row, 0)


def conv_weights(out_ref, w_ref):
    zero = jnp.zeros((128, 128), BF16)
    for i in range(3):
        for j in range(4):
            left = w_ref[3 * i + j] if j < 3 else zero
            right = w_ref[3 * i + j - 1] if j > 0 else zero
            start = (4 * i + j) * 128
            out_ref[start : start + 128, :] = jnp.concatenate([left, right], axis=1)


def conv_pair(a_ref, w, pair, start, rows):
    parts = []
    for i in range(3):
        for j in range(4):
            parts.append(a_ref[2 * pair + j, pl.ds(start + i * B, rows), :])
    return dot(jnp.concatenate(parts, axis=1), w)


def kernel(
    noisy_ref,
    vec_ref,
    gain_ref,
    seam_ref,
    key_ref,
    blk_ref,
    wl_ref,
    wf_ref,
    wc_ref,
    wo_ref,
    den_ref,
    stat_ref,
    nx,
    sx,
    lift_w,
    out_w,
    fine_w,
    coarse_w,
    ones_ref,
    perm_a,
    perm_b,
    perm_c,
    slot_ref,
    sum_ref,
    halo,
    started,
    a1,
    fine,
    pooled,
    a2,
    halo2,
    coarse,
    d_ref,
    send,
    recv,
    tgt,
    mrecv,
    gat,
    h_send,
    h_recv,
    c_send,
    c_recv,
    a_send,
    a_recv,
    m_send,
    m_recv,
    g_send,
    g_recv,
):
    pos = lax.axis_index("tile")
    mem = lax.axis_index("mem")
    east = lax.rem(pos + 1, NT)
    west = lax.rem(pos + NT - 1, NT)

    barrier = pltpu.get_barrier_semaphore()

    def greet_tile(d, _):
        pl.semaphore_signal(
            barrier, inc=1, device_id={"tile": lax.rem(pos + d, NT)}, device_id_type=MESH
        )
        return 0

    def greet_mem(d, _):
        pl.semaphore_signal(
            barrier, inc=1, device_id={"mem": lax.rem(mem + d, NM)}, device_id_type=MESH
        )
        return 0

    lax.fori_loop(1, NT, greet_tile, 0)
    lax.fori_loop(1, NM, greet_mem, 0)
    pl.semaphore_wait(barrier, NT - 1 + NM - 1)

    to_west = pltpu.make_async_remote_copy(
        src_ref=noisy_ref.at[:, pl.ds(0, 128)],
        dst_ref=halo.at[0],
        send_sem=h_send.at[0],
        recv_sem=h_recv.at[0],
        device_id={"tile": west},
        device_id_type=MESH,
    )
    to_east = pltpu.make_async_remote_copy(
        src_ref=noisy_ref.at[:, pl.ds(128, 128)],
        dst_ref=halo.at[1],
        send_sem=h_send.at[1],
        recv_sem=h_recv.at[1],
        device_id={"tile": east},
        device_id_type=MESH,
    )
    to_west.start()
    to_east.start()

    c_in, c_skip, c_out = twice(vec_ref[0]), twice(vec_ref[1]), twice(vec_ref[2])
    temb, frac_p, frac_q = twice(vec_ref[3]), twice(vec_ref[4]), twice(vec_ref[5])
    gain_fine = twice(gain_ref[0:1]) * 0.5
    gain_coarse = gain_ref[1:2] * 0.5
    gain_out = twice(gain_ref[2:3]) * 0.5

    def lift_row(r, _):
        lane = iota((B, 512), 1)
        want = iota((B, 512), 0) * N + r
        perm_a[pl.ds(pl.multiple_of(r * B, B), B), :] = jnp.where(want == lane, 1.0, 0.0).astype(
            BF16
        )
        return 0

    lax.fori_loop(0, N, lift_row, 0)
    ones_ref[...] = jnp.where(
        iota((256, 256), 0) // 128 == iota((256, 256), 1) // 128, 1.0 / 128, 0.0
    ).astype(BF16)
    wl = wl_ref[...].astype(F32)
    wl_zero = jnp.zeros_like(wl)
    wl_pair = jnp.concatenate(
        [
            jnp.concatenate([wl, wl_zero], axis=1),
            jnp.concatenate([wl_zero, wl], axis=1),
        ],
        axis=0,
    ).astype(BF16)
    for q in range(8):
        lift_w[q] = jnp.zeros((128, 256), BF16)
        lift_w[q, q * B : (q + 1) * B, :] = wl_pair
        for j in range(2):
            place = jnp.where(
                iota((8, 128), 1) == iota((8, 128), 0) + (16 * q + 8 * j), 1.0, 0.0
            ).astype(BF16)
            out_w[q, j * 128 : (j + 1) * 128, :] = dot(wo_ref[...], place).astype(BF16)
    conv_weights(fine_w, wf_ref)
    conv_weights(coarse_w, wc_ref)

    natural = noisy_ref[...]
    for s in range(2):
        rows = slice(s * 256, (s + 1) * 256)
        moved = dot(perm_a[rows, :], natural)
        nx[rows, :] = moved.astype(BF16)
        sx[rows, :] = (moved.reshape(H, B, 256) * c_in).reshape(256, 256).astype(BF16)

    def lift(q, _):
        for half in range(2):
            pair = half * 8 + q
            for s in range(2):
                rows = slice(s * 256, (s + 1) * 256)
                up = dot(sx[rows, half * 128 : (half + 1) * 128], lift_w[q])
                first = (up.reshape(H, B, 256) + temb).reshape(256, 256).astype(BF16)
                started[2 * pair, rows, :] = first[:, :128]
                started[2 * pair + 1, rows, :] = first[:, 128:]
                normed = act(first.astype(F32), ones_ref[...], gain_fine)
                inner = slice(s * 256 + B, (s + 1) * 256 + B)
                a1[2 * pair + 1, inner, :] = normed[:, :128]
                a1[2 * pair + 2, inner, :] = normed[:, 128:]
        return 0

    lax.fori_loop(0, 8, lift, 0)

    def north_south(a_ref, perm, n, row_from, row_to):
        edge = a_ref[1 : n + 1, row_from * B : (row_from + 1) * B, :].reshape(n * B, 128)
        got = dot(perm[...], edge).astype(BF16).reshape(n, B, 128)
        rows = slice(row_to * B, (row_to + 1) * B)
        a_ref[1 : n + 1, rows, :] = got
        a_ref[0, rows, :] = got[0]
        a_ref[n + 1, rows, :] = got[n - 1]

    seam_perm(perm_a, seam_ref, 0, N, False)
    north_south(a1, perm_a, N, N, 0)
    seam_perm(perm_b, seam_ref, 2, N, False)
    north_south(a1, perm_b, N, 1, N + 1)
    seam_perm(perm_a, seam_ref, 1, N, True)
    seam_perm(perm_b, seam_ref, 3, N, True)
    to_west.wait()
    to_east.wait()
    for s in range(2):
        rows = slice(s * 256, (s + 1) * 256)
        sides = []
        for perm, side, w in (
            (perm_b, 1, lift_w[7, :, 128:256]),
            (perm_a, 0, lift_w[0, :, 0:128]),
        ):
            moved = dot(perm[rows, :], halo[side])
            scaled = (moved.reshape(H, B, 128) * vec_ref[0]).reshape(256, 128).astype(BF16)
            sides.append(dot(scaled, w))
        up = jnp.concatenate(sides, axis=1)
        first = (up.reshape(H, B, 256) + temb).reshape(256, 256).astype(BF16)
        normed = act(first.astype(F32), ones_ref[...], gain_fine)
        inner = slice(s * 256 + B, (s + 1) * 256 + B)
        a1[0, inner, :] = normed[:, :128]
        a1[N + 1, inner, :] = normed[:, 128:]

    def fine_pair(pair):
        for s in range(2):
            rows = slice(s * 256, (s + 1) * 256)
            got = conv_pair(a1, fine_w[...], pair, s * 256, 256)
            base = jnp.concatenate([started[2 * pair, rows, :], started[2 * pair + 1, rows, :]], axis=1)
            out = (base.astype(F32) + got).astype(BF16)
            fine[2 * pair, rows, :] = out[:, :128]
            fine[2 * pair + 1, rows, :] = out[:, 128:]
            wide = out.astype(F32).reshape(H // 2, 2, B, 256)
            tall = wide[:, 0] + wide[:, 1]
            mean = ((tall[:, :, :128] + tall[:, :, 128:]) * 0.25).reshape(128, 128).astype(BF16)
            half_rows = slice(s * 128, (s + 1) * 128)
            pooled[pair, half_rows, :] = mean
            normed = act(mean.astype(F32), ones_ref[0:128, 0:128], gain_coarse)
            a2[pair + 1, s * 128 + B : (s + 1) * 128 + B, :] = normed

    fine_pair(0)
    fine_pair(H - 1)
    c_west = pltpu.make_async_remote_copy(
        src_ref=a2.at[1, pl.ds(B, 256)],
        dst_ref=halo2.at[0],
        send_sem=c_send.at[0],
        recv_sem=c_recv.at[0],
        device_id={"tile": west},
        device_id_type=MESH,
    )
    c_east = pltpu.make_async_remote_copy(
        src_ref=a2.at[H, pl.ds(B, 256)],
        dst_ref=halo2.at[1],
        send_sem=c_send.at[1],
        recv_sem=c_recv.at[1],
        device_id={"tile": east},
        device_id_type=MESH,
    )
    c_west.start()
    c_east.start()

    def fine_loop(pair, _):
        fine_pair(pair)
        return 0

    lax.fori_loop(1, H - 1, fine_loop, 0)

    seam_perm(perm_c, seam_ref, 0, H, False)
    north_south(a2, perm_c, H, H, 0)
    seam_perm(perm_c, seam_ref, 2, H, False)
    north_south(a2, perm_c, H, 1, H + 1)
    c_west.wait()
    c_east.wait()
    seam_perm(perm_c, seam_ref, 1, H, False)
    a2[H + 1, B : B + 256, :] = dot(perm_c[...], halo2[0]).astype(BF16)
    seam_perm(perm_c, seam_ref, 3, H, False)
    a2[0, B : B + 256, :] = dot(perm_c[...], halo2[1]).astype(BF16)

    def coarse_loop(pair, _):
        got = conv_pair(a2, coarse_w[...], pair, 0, 256)
        base = jnp.concatenate([pooled[2 * pair], pooled[2 * pair + 1]], axis=1)
        out = (base.astype(F32) + got).astype(BF16)
        coarse[2 * pair] = out[:, :128]
        coarse[2 * pair + 1] = out[:, 128:]
        return 0

    lax.fori_loop(0, H // 2, coarse_loop, 0)

    i, j = iota((512, 128), 0), iota((512, 128), 1)
    slot_ref[...] = jnp.where(
        ((i >> 4) == key_ref[...]) & (((i >> 3) & 1) == ((j >> 3) & 1)) & ((i & 7) == (j >> 4)),
        1.0,
        0.0,
    ).astype(BF16)
    i, j = iota((64, 512), 0), iota((64, 512), 1)
    sum_ref[...] = jnp.where(
        ((i & 3) == blk_ref[...]) & (((i >> 2) & 1) == ((j >> 3) & 1)) & ((i >> 3) == (j & 7)),
        1.0,
        0.0,
    ).astype(BF16)

    rows_c = RC * B

    def a_copy(k, d):
        return pltpu.make_async_remote_copy(
            src_ref=send.at[k, d],
            dst_ref=recv.at[k, d],
            send_sem=a_send.at[k, d],
            recv_sem=a_recv.at[k, d],
            device_id={"tile": lax.rem(pos + d, NT)},
            device_id_type=MESH,
        )

    def m_copy(k, d):
        return pltpu.make_async_remote_copy(
            src_ref=tgt.at[k, lax.rem(mem + d, NM)],
            dst_ref=mrecv.at[k, d],
            send_sem=m_send.at[k, d],
            recv_sem=m_recv.at[k, d],
            device_id={"mem": lax.rem(mem + d, NM)},
            device_id_type=MESH,
        )

    def g_copy(k, d):
        return pltpu.make_async_remote_copy(
            src_ref=gat.at[k, mem],
            dst_ref=gat.at[k, mem],
            send_sem=g_send.at[k, d],
            recv_sem=g_recv.at[k, d],
            device_id={"mem": lax.rem(mem + d, NM)},
            device_id_type=MESH,
        )

    def each(count, what):
        def body(d, _):
            what(d)
            return 0

        lax.fori_loop(1, count, body, 0)

    def last_stage(k):
        start = k * rows_c

        def pair_step(q, sums):
            out = []
            for half in range(2):
                pair = half * 8 + q
                f = jnp.concatenate(
                    [fine[2 * pair, start : start + rows_c, :], fine[2 * pair + 1, start : start + rows_c, :]],
                    axis=1,
                ).astype(F32)
                c = coarse[pair, start // 2 : (start + rows_c) // 2, :].astype(F32)
                c = c.reshape(RC // 2, 1, B, 128)
                c = jnp.concatenate([c, c], axis=1).reshape(rows_c, 128)
                normed = act(f + twice(c), ones_ref[...], gain_out)
                out.append(sums[half] + dot(normed, out_w[q]))
            return tuple(out)

        zero = jnp.zeros((rows_c, 128), F32)
        left, right = lax.fori_loop(0, 8, pair_step, (zero, zero))
        proj = jnp.concatenate([left, right], axis=1).reshape(RC, B, 256)
        state = nx[start : start + rows_c, :].astype(F32).reshape(RC, B, 256)
        den = (c_skip * state + c_out * proj).reshape(rows_c, 256)
        d_ref[start : start + rows_c, :] = den
        den_ref[start : start + rows_c, :] = den
        if k == CH - 1:
            d_ref[N * B : (N + 1) * B, :] = den[rows_c - B :, :]
        below = d_ref[start + B : start + B + rows_c, :].reshape(RC, B, 256)
        mixed = (1.0 - frac_p) * den.reshape(RC, B, 256) + frac_p * below
        mixed = mixed.reshape(rows_c, 256)
        shifted = pltpu.roll(mixed, 248, 1)
        shifted = jnp.where(iota((rows_c, 256), 1) >= 248, mixed, shifted)
        out = (1.0 - frac_q) * mixed.reshape(RC, B, 256) + frac_q * shifted.reshape(RC, B, 256)
        blocks = dot(slot_ref[...], out.reshape(rows_c, 256).astype(BF16)).astype(BF16)
        blocks = blocks.reshape(NT, 32, 256)
        recv[k, 0] = blocks[0]
        send[k] = blocks
        each(NT, lambda d: a_copy(k, d).start())

    def sum_stage(k):
        each(NT, lambda d: a_copy(k, d).wait_recv())
        total = dot(sum_ref[...], recv[k].reshape(512, 256))
        tgt[k] = total.reshape(NM, 8, 256)
        mrecv[k, 0] = tgt[k, mem]
        each(NM, lambda d: m_copy(k, d).start())

    def stat_stage(k):
        each(NM, lambda d: m_copy(k, d).wait_recv())
        values = mrecv[k]
        total = jnp.sum(values, axis=0)
        mean = (total[0:4] + total[4:8]) * (1.0 / 16)
        dev = values - jnp.concatenate([mean, mean], axis=0)
        squares = jnp.sum(dev * dev, axis=0)
        spread = jnp.sqrt((squares[0:4] + squares[4:8]) / 15.0 + 1e-06)
        gat[k, mem] = jnp.concatenate([mean, spread], axis=0)
        each(NM, lambda d: g_copy(k, d).start())

    order = list(range(CH - 1, -1, -1))
    for step in range(CH + 2):
        if step < CH:
            last_stage(order[step])
        if 1 <= step < CH + 1:
            sum_stage(order[step - 1])
        if 2 <= step:
            stat_stage(order[step - 2])
    for k in order:
        each(NM, lambda d: g_copy(k, d).wait_recv())
    stat_ref[...] = gat[...]
    for k in order:
        each(NT, lambda d: a_copy(k, d).wait_send())
        each(NM, lambda d: m_copy(k, d).wait_send())
        each(NM, lambda d: g_copy(k, d).wait_send())


def precondition(timestep):
    fraction = timestep.astype(jnp.float32) / (STEPS - 1)
    high_root = 80.0 ** (1.0 / 7.0)
    low_root = 0.002 ** (1.0 / 7.0)
    sigma = (high_root + fraction * (low_root - high_root)) ** 7
    denominator = sigma * sigma + 1.0
    return (lax.rsqrt(denominator), 1.0 / denominator, sigma * lax.rsqrt(denominator))


def embed(timestep, w_time):
    half_width = w_time.shape[0] // 2
    frequency = jnp.exp(-math.log(10000.0) * jnp.arange(half_width, dtype=jnp.float32) / half_width)
    angles = timestep.astype(jnp.float32)[:, None] * frequency[None, :]
    features = jnp.concatenate([jnp.sin(angles), jnp.cos(angles)], axis=-1)
    return jax.nn.silu(jnp.dot(features, w_time, precision=lax.Precision.HIGHEST))


def on_device(
    noisy,
    timestep,
    seams,
    corner_list,
    route,
    target_block,
    frac,
    w_time,
    w_lift,
    w_fine,
    w_coarse,
    gain_fine,
    gain_coarse,
    gain_out,
    w_out,
):
    pos = lax.axis_index("tile")
    scales = precondition(timestep)
    temb = embed(timestep, w_time)

    def rows(x):
        return jnp.broadcast_to(jnp.repeat(x, 8)[:, None], (B, 128))

    def tiles(x):
        return jnp.broadcast_to(jnp.concatenate([x, x])[:, None], (B, 128))

    vec = jnp.stack(
        [rows(s) for s in scales]
        + [jnp.repeat(temb, 8, axis=0), tiles(frac[:, 0]), tiles(frac[:, 1])]
    )
    gains = jnp.stack([gain_fine, gain_coarse, gain_out])
    seam = seams.reshape(8, 12)
    seam = jnp.concatenate([seam, seam], axis=0)

    owners = route.reshape(NT, 8)
    same = owners[:, :, None] == owners[:, None, :]
    earlier = jnp.arange(8)[None, :, None] > jnp.arange(8)[None, None, :]
    rank = jnp.sum((same & earlier).astype(jnp.int32), axis=2)
    own_owner = lax.dynamic_index_in_dim(owners, pos, 0, False)
    own_rank = lax.dynamic_index_in_dim(rank, pos, 0, False)
    key = (own_owner - pos) % NT * 2 + own_rank
    key_lane = jnp.tile(key, 16)[None, :]
    blocks = target_block.reshape(NT, 8)
    mine = (owners == pos)[:, None, :] & (rank[:, None, :] == jnp.arange(2)[None, :, None])
    slot_block = jnp.max(jnp.where(mine, blocks[:, None, :], -1), axis=2)
    slot_block = jnp.take(slot_block, (pos - jnp.arange(NT)) % NT, axis=0)
    blk_lane = jnp.repeat(slot_block.reshape(32), 16)[None, :]

    vmem = pl.BlockSpec(memory_space=pltpu.VMEM)
    dma = pltpu.SemaphoreType.DMA
    den, stat = pl.pallas_call(
        kernel,
        out_shape=(
            jax.ShapeDtypeStruct((512, 256), F32),
            jax.ShapeDtypeStruct((CH, NM, 8, 256), F32),
        ),
        in_specs=[vmem] * 10,
        out_specs=(vmem, vmem),
        scratch_shapes=[
            pltpu.VMEM((512, 256), BF16),
            pltpu.VMEM((512, 256), BF16),
            pltpu.VMEM((8, 128, 256), BF16),
            pltpu.VMEM((8, 256, 128), BF16),
            pltpu.VMEM((1536, 256), BF16),
            pltpu.VMEM((1536, 256), BF16),
            pltpu.VMEM((256, 256), BF16),
            pltpu.VMEM((512, 512), BF16),
            pltpu.VMEM((512, 512), BF16),
            pltpu.VMEM((256, 256), BF16),
            pltpu.VMEM((512, 128), BF16),
            pltpu.VMEM((64, 512), BF16),
            pltpu.VMEM((2, 512, 128), BF16),
            pltpu.VMEM((N, 512, 128), BF16),
            pltpu.VMEM((N + 2, 544, 128), BF16),
            pltpu.VMEM((N, 512, 128), BF16),
            pltpu.VMEM((H, 256, 128), BF16),
            pltpu.VMEM((H + 2, 288, 128), BF16),
            pltpu.VMEM((2, 256, 128), BF16),
            pltpu.VMEM((H, 256, 128), BF16),
            pltpu.VMEM(((N + 1) * B, 256), F32),
            pltpu.VMEM((CH, NT, 32, 256), BF16),
            pltpu.VMEM((CH, NT, 32, 256), BF16),
            pltpu.VMEM((CH, NM, 8, 256), F32),
            pltpu.VMEM((CH, NM, 8, 256), F32),
            pltpu.VMEM((CH, NM, 8, 256), F32),
            dma((2,)),
            dma((2,)),
            dma((2,)),
            dma((2,)),
            dma((CH, NT)),
            dma((CH, NT)),
            dma((CH, NM)),
            dma((CH, NM)),
            dma((CH, NM)),
            dma((CH, NM)),
        ],
        compiler_params=pltpu.CompilerParams(
            collective_id=0, has_side_effects=True, vmem_limit_bytes=56 * 1024 * 1024
        ),
    )(
        noisy.reshape(512, 256),
        vec,
        gains,
        seam,
        key_lane,
        blk_lane,
        w_lift,
        w_fine,
        w_coarse,
        w_out,
    )
    denoised = den.reshape(N, B, 256).transpose(1, 0, 2).reshape(noisy.shape)
    stat = stat.reshape(N, 2, 4, 256)
    ens_mean = stat[:, 0].transpose(1, 0, 2)
    ens_spread = stat[:, 1].transpose(1, 0, 2)
    return (denoised, ens_mean, ens_spread)


def solution(mesh):
    placed = (
        P("mem", "tile", None, None),
        P("mem"),
        P("tile", None, None),
        P("tile", None, None),
        P(),
        P(),
        P("tile", None),
        P(),
        P(),
        P(),
        P(),
        P(),
        P(),
        P(),
        P(),
    )
    return jax.shard_map(
        on_device,
        mesh=mesh,
        in_specs=placed,
        out_specs=(P("mem", "tile", None, None), P("tile", None, None), P("tile", None, None)),
        check_vma=False,
    )
```

time: 434 us -> 119 us (0.27); the launches traced: 428 us -> 118 us
  waiting for transfers between devices: 233 us -> 0 us
  Pallas kernels: 0 us -> 104 us
  other arithmetic: 70.3 us -> 2.51 us
  local copies, waits for them, and re-layouts: 60.3 us -> 10.4 us
  matrix products: 36 us -> 0.22 us
  between operations: 15.5 us -> 0.76 us
  starting transfers between devices: 12.1 us -> 0 us
    psum x2 -> x0, waiting for transfers between devices: 115 us -> none  [the longest x1 58 us: on_device(): summed = lax.psum(jnp.sum(target, axis=0), 'mem')]
    unnamed x4 -> x0, waiting for transfers between devices: 105 us -> none
    pallas_call x0 -> x1, Pallas kernels: none -> 104 us  [on_device(): pl.pallas_call(kernel, out_shape=(jax.ShapeDtypeStruct((512, 256), F32),...]
    dot_general x21 -> x0, matrix products: 35.8 us -> none  [the longest x18 23.8 us: convolve(): jnp.dot(slab_view, weight[3 * row_off + col_off], preferred_element_type=...]
    reduce_sum x5 -> x1, other arithmetic: 25 us -> 0.09 us  [on_device(): rank = jnp.sum((same & earlier).astype(jnp.int32), axis=2)]
    concatenate x7 -> x2, other arithmetic: 19 us -> 0.68 us  [the longest x1 0.6 us: on_device(): seam = jnp.concatenate([seam, seam], axis=0)]
    slice x15 -> x0, local copies, waits for them, and re-layouts: 15.9 us -> none  [the longest x4 13.7 us: convolve(): padded[:, :, row_off:row_off + edge_len, col_off:col_off + edge_len]]
    convert_element_type x5 -> x0, other arithmetic: 14.9 us -> none  [the longest x3 9.33 us: rms_act(): return jax.nn.silu(normed).astype(jnp.bfloat16)]
  transfers between devices with their start and end apart: 7 -> 0, of which waited for: 5 -> 0; matrix products, arithmetic and copies ran while one was open for 1% -> 0% of each run, Pallas kernels for 0% -> 0%
where the time goes in v1:
time: 119 us; the launch traced here: 118 us
  Pallas kernels  104 us (87%)
  local copies, waits for them, and re-layouts  10.4 us (9%)
  other arithmetic  2.51 us (2%)
    pallas_call x1, Pallas kernels, on_device(): pl.pallas_call(kernel, out_shape=(jax.ShapeDtypeStruct((512, 256), F32),...  104 us
    unnamed x31, local copies, waits for them, and re-layouts  4.15 us

profile of v1, /device:TPU:1, one launch (start us, length us, event | category | flops | bytes accessed | tf_op | source)
XLA Modules:
  0.0 118.3 jit_solution(597199865455177169)
XLA Ops:
  0.7 0.5 broadcast.182
  1.2 0.2 copy-done.10
  1.3 0.7 reduce.5
  2.0 0.6 copy-done.11
  2.7 0.1 multiply_sine_fusion
  2.8 0.2 divide_multiply_fusion
  3.1 0.5 copy-done.5
  3.7 0.1 stack_broadcast_in_dim.35
  4.1 0.6 copy-done.6
  4.7 0.6 pad_maximum_fusion.gain_ref
  5.5 0.1 convert_reduce_fusion
  5.6 0.2 fusion.4
  5.9 0.7 broadcast_in_dim_tile.3.key_ref
  6.8 0.6 gather_fusion
  7.4 0.1 select_n.66
  7.6 0.7 broadcast_in_dim_reshape.2.blk_ref
  8.3 0.1 copy.57
  8.5 0.6 pad_add_fusion.seam_ref
  9.2 0.7 copy.53.wo_ref
  10.2 0.6 copy-done.2
  10.9 104.4 %shard_map.157 = (f32[512,256]{1,0:T(8,128)}, f32[4,8,8,256]{3,2,1,0:T(8,128)}) custom-call(bf16[512,256]{1,0:T(8,128)(2,1)} %bitcast.30, f32[6,16,128]{2,1,0:T(8,128)} %copy-done.2, f32[3,128]{1,0:T(4,128)} %pad_maximum_fusion.gain_ref, s32[16,12]{1,0:T(8,128)} %pad_add_fusion.seam_ref, s32[1,128]{1,0:T(1,128)} %broadcast_in_dim_tile.3.key_ref, ...), custom_call_target="tpu_custom_call" | custom-call | tf_op jit(solution)/shard_map/pallas_call | solution.py:523
  115.3 2.2 %copy.54 = f32[16,32,256]{2,1,0:T(8,128)} copy(f32[16,32,256]{2,0,1:T(8,128)} %bitcast.29) | data formatting | bytes 1048576 | tf_op jit(solution)/shard_map/transpose | solution.py:584
  117.5 0.1 copy.58
  117.5 0.7 slice_bitcast_fusion
  (52 shorter events, 1.8 us)
Async XLA Ops:
  0.6 2.2 %copy-start = (f32[128,128]{1,0:T(8,128)S(1)}, f32[128,128]{1,0:T(8,128)}, u32[]{:S(2)}) copy-start(f32[128,128]{1,0:T(8,128)} %param.21) | copy-start | bytes 196612
  0.6 0.7 copy-start.10
  2.0 0.7 copy-start.11
  2.8 0.7 copy-start.5
  4.0 0.7 copy-start.6
  4.0 0.7 copy-start.7
  4.0 0.7 copy-start.8
  5.8 0.7 copy-start.9
  7.6 0.7 copy-start.3
  8.5 0.7 copy-start.4
  10.2 0.6 copy-start.2
  115.3 2.2 %copy-start.1 = (f32[4,8,8,256]{3,2,1,0:T(8,128)S(1)}, f32[4,8,8,256]{3,2,1,0:T(8,128)}, u32[]{:S(2)}) copy-start(f32[4,8,8,256]{3,2,1,0:T(8,128)} %get-tuple-element.6) | copy-start | bytes 786436

commit v2 on v1

--- a/solution.py
+++ b/solution.py
@@ -40,21 +40,21 @@
     return (h + h * jnp.tanh(h)).astype(BF16)
 
 
-def seam_perm(perm_ref, seam_ref, side, n, natural):
-    tile = seam_ref[:, 3 * side : 3 * side + 1] % 8
-    flag = seam_ref[:, 3 * side + 2 : 3 * side + 3]
-    base = (iota((B, 1), 0) // 8) * 8 + tile
-    lane = iota((B, n * B), 1)
-
-    def row(r, _):
-        along = jnp.where(flag == 1, n - 1 - r, r)
-        source = base * n + along if natural else along * B + base
-        perm_ref[pl.ds(pl.multiple_of(r * B, B), B), :] = jnp.where(
-            source == lane, 1.0, 0.0
-        ).astype(BF16)
-        return 0
-
-    lax.fori_loop(0, n, row, 0)
+def seam_perm(out_ref, seam_ref, side):
+    tile = seam_ref[:, 3 * side : 3 * side + 1] & 7
+    apart = iota((B, 256), 1) - ((iota((B, 256), 0) & 8) + tile)
+    for c in range(256 // B):
+        out_ref[side, c * B : (c + 1) * B, :] = jnp.where(apart == c * B, 1.0, 0.0).astype(BF16)
+
+
+def from_side(perm, edge, n, flipped):
+    if n * B > 256:
+        edge = jnp.concatenate([edge[:256], edge[256:]], axis=1)
+    got = dot(perm, edge)
+    pieces = [
+        got[c % H * B : (c % H + 1) * B, c // H * 128 : (c // H + 1) * 128] for c in range(n)
+    ]
+    return [jnp.where(flipped, pieces[n - 1 - c], pieces[c]) for c in range(n)]
 
 
 def conv_weights(out_ref, w_ref):
@@ -95,9 +95,8 @@
     fine_w,
     coarse_w,
     ones_ref,
-    perm_a,
-    perm_b,
-    perm_c,
+    to_rows,
+    seam_w,
     slot_ref,
     sum_ref,
     halo,
@@ -108,6 +107,10 @@
     a2,
     halo2,
     coarse,
+    g0,
+    g1,
+    act_s,
+    edges,
     d_ref,
     send,
     recv,
@@ -148,25 +151,6 @@
     lax.fori_loop(1, NM, greet_mem, 0)
     pl.semaphore_wait(barrier, NT - 1 + NM - 1)
 
-    to_west = pltpu.make_async_remote_copy(
-        src_ref=noisy_ref.at[:, pl.ds(0, 128)],
-        dst_ref=halo.at[0],
-        send_sem=h_send.at[0],
-        recv_sem=h_recv.at[0],
-        device_id={"tile": west},
-        device_id_type=MESH,
-    )
-    to_east = pltpu.make_async_remote_copy(
-        src_ref=noisy_ref.at[:, pl.ds(128, 128)],
-        dst_ref=halo.at[1],
-        send_sem=h_send.at[1],
-        recv_sem=h_recv.at[1],
-        device_id={"tile": east},
-        device_id_type=MESH,
-    )
-    to_west.start()
-    to_east.start()
-
     c_in, c_skip, c_out = twice(vec_ref[0]), twice(vec_ref[1]), twice(vec_ref[2])
     temb, frac_p, frac_q = twice(vec_ref[3]), twice(vec_ref[4]), twice(vec_ref[5])
     gain_fine = twice(gain_ref[0:1]) * 0.5
@@ -176,7 +160,7 @@
     def lift_row(r, _):
         lane = iota((B, 512), 1)
         want = iota((B, 512), 0) * N + r
-        perm_a[pl.ds(pl.multiple_of(r * B, B), B), :] = jnp.where(want == lane, 1.0, 0.0).astype(
+        to_rows[pl.ds(pl.multiple_of(r * B, B), B), :] = jnp.where(want == lane, 1.0, 0.0).astype(
             BF16
         )
         return 0
@@ -201,87 +185,118 @@
             place = jnp.where(
                 iota((8, 128), 1) == iota((8, 128), 0) + (16 * q + 8 * j), 1.0, 0.0
             ).astype(BF16)
-            out_w[q, j * 128 : (j + 1) * 128, :] = dot(wo_ref[...], place).astype(BF16)
+            out_w[(2 * q + j) * 128 : (2 * q + j + 1) * 128, :] = dot(wo_ref[...], place).astype(BF16)
+    for side in range(4):
+        seam_perm(seam_w, seam_ref, side)
+    flipped = [
+        jnp.broadcast_to(seam_ref[:, 3 * side + 2 : 3 * side + 3], (B, 128)) == 1
+        for side in range(4)
+    ]
     conv_weights(fine_w, wf_ref)
     conv_weights(coarse_w, wc_ref)
 
     natural = noisy_ref[...]
     for s in range(2):
         rows = slice(s * 256, (s + 1) * 256)
-        moved = dot(perm_a[rows, :], natural)
+        moved = dot(to_rows[rows, :], natural)
         nx[rows, :] = moved.astype(BF16)
         sx[rows, :] = (moved.reshape(H, B, 256) * c_in).reshape(256, 256).astype(BF16)
 
-    def lift(q, _):
-        for half in range(2):
-            pair = half * 8 + q
-            for s in range(2):
-                rows = slice(s * 256, (s + 1) * 256)
-                up = dot(sx[rows, half * 128 : (half + 1) * 128], lift_w[q])
-                first = (up.reshape(H, B, 256) + temb).reshape(256, 256).astype(BF16)
-                started[2 * pair, rows, :] = first[:, :128]
-                started[2 * pair + 1, rows, :] = first[:, 128:]
-                normed = act(first.astype(F32), ones_ref[...], gain_fine)
-                inner = slice(s * 256 + B, (s + 1) * 256 + B)
-                a1[2 * pair + 1, inner, :] = normed[:, :128]
-                a1[2 * pair + 2, inner, :] = normed[:, 128:]
+    to_west = pltpu.make_async_remote_copy(
+        src_ref=nx.at[:, pl.ds(0, 128)],
+        dst_ref=halo.at[0],
+        send_sem=h_send.at[0],
+        recv_sem=h_recv.at[0],
+        device_id={"tile": west},
+        device_id_type=MESH,
+    )
+    to_east = pltpu.make_async_remote_copy(
+        src_ref=nx.at[:, pl.ds(128, 128)],
+        dst_ref=halo.at[1],
+        send_sem=h_send.at[1],
+        recv_sem=h_recv.at[1],
+        device_id={"tile": east},
+        device_id_type=MESH,
+    )
+    to_west.start()
+    to_east.start()
+
+    def lift(step, _):
+        for q in (2 * step, 2 * step + 1):
+            for half in range(2):
+                pair = half * 8 + q
+                for s in range(2):
+                    rows = slice(s * 256, (s + 1) * 256)
+                    up = dot(sx[rows, half * 128 : (half + 1) * 128], lift_w[q])
+                    first = (up.reshape(H, B, 256) + temb).reshape(256, 256).astype(BF16)
+                    started[2 * pair, rows, :] = first[:, :128]
+                    started[2 * pair + 1, rows, :] = first[:, 128:]
+                    normed = act(first.astype(F32), ones_ref[...], gain_fine)
+                    inner = slice(s * 256 + B, (s + 1) * 256 + B)
+                    a1[2 * pair + 1, inner, :] = normed[:, :128]
+                    a1[2 * pair + 2, inner, :] = normed[:, 128:]
         return 0
 
-    lax.fori_loop(0, 8, lift, 0)
-
-    def north_south(a_ref, perm, n, row_from, row_to):
+    lax.fori_loop(0, 4, lift, 0)
+
+    def north_south(a_ref, side, n, row_from, row_to):
         edge = a_ref[1 : n + 1, row_from * B : (row_from + 1) * B, :].reshape(n * B, 128)
-        got = dot(perm[...], edge).astype(BF16).reshape(n, B, 128)
+        got = from_side(seam_w[side], edge, n, flipped[side])
         rows = slice(row_to * B, (row_to + 1) * B)
-        a_ref[1 : n + 1, rows, :] = got
-        a_ref[0, rows, :] = got[0]
-        a_ref[n + 1, rows, :] = got[n - 1]
-
-    seam_perm(perm_a, seam_ref, 0, N, False)
-    north_south(a1, perm_a, N, N, 0)
-    seam_perm(perm_b, seam_ref, 2, N, False)
-    north_south(a1, perm_b, N, 1, N + 1)
-    seam_perm(perm_a, seam_ref, 1, N, True)
-    seam_perm(perm_b, seam_ref, 3, N, True)
+        for c in range(n):
+            a_ref[c + 1, rows, :] = got[c].astype(BF16)
+        a_ref[0, rows, :] = got[0].astype(BF16)
+        a_ref[n + 1, rows, :] = got[n - 1].astype(BF16)
+
+    north_south(a1, 0, N, N, 0)
+    north_south(a1, 2, N, 1, N + 1)
     to_west.wait()
     to_east.wait()
-    for s in range(2):
-        rows = slice(s * 256, (s + 1) * 256)
-        sides = []
-        for perm, side, w in (
-            (perm_b, 1, lift_w[7, :, 128:256]),
-            (perm_a, 0, lift_w[0, :, 0:128]),
-        ):
-            moved = dot(perm[rows, :], halo[side])
-            scaled = (moved.reshape(H, B, 128) * vec_ref[0]).reshape(256, 128).astype(BF16)
-            sides.append(dot(scaled, w))
-        up = jnp.concatenate(sides, axis=1)
-        first = (up.reshape(H, B, 256) + temb).reshape(256, 256).astype(BF16)
-        normed = act(first.astype(F32), ones_ref[...], gain_fine)
-        inner = slice(s * 256 + B, (s + 1) * 256 + B)
-        a1[0, inner, :] = normed[:, :128]
-        a1[N + 1, inner, :] = normed[:, 128:]
-
-    def fine_pair(pair):
+    sides = []
+    for side, got, w in ((3, 1, lift_w[7, :, 128:256]), (1, 0, lift_w[0, :, 0:128])):
+        moved = from_side(seam_w[side], halo[got], N, flipped[side])
+        scaled = jnp.concatenate([(x * vec_ref[0]).astype(BF16) for x in moved], axis=0)
+        sides.append(dot(scaled, w))
+    up = jnp.concatenate(sides, axis=1)
+    first = (up.reshape(N, B, 256) + temb).reshape(512, 256).astype(BF16)
+    normed = act(first.astype(F32), ones_ref[...], gain_fine)
+    a1[0, B : B + 512, :] = normed[:, :128]
+    a1[N + 1, B : B + 512, :] = normed[:, 128:]
+
+    def fine_conv(pair, buf):
+        for s in range(2):
+            buf[s * 256 : (s + 1) * 256, :] = conv_pair(a1, fine_w[...], pair, s * 256, 256)
+
+    def fine_post(pair, buf):
         for s in range(2):
             rows = slice(s * 256, (s + 1) * 256)
-            got = conv_pair(a1, fine_w[...], pair, s * 256, 256)
             base = jnp.concatenate([started[2 * pair, rows, :], started[2 * pair + 1, rows, :]], axis=1)
-            out = (base.astype(F32) + got).astype(BF16)
+            out = (base.astype(F32) + buf[rows, :]).astype(BF16)
             fine[2 * pair, rows, :] = out[:, :128]
             fine[2 * pair + 1, rows, :] = out[:, 128:]
             wide = out.astype(F32).reshape(H // 2, 2, B, 256)
             tall = wide[:, 0] + wide[:, 1]
             mean = ((tall[:, :, :128] + tall[:, :, 128:]) * 0.25).reshape(128, 128).astype(BF16)
-            half_rows = slice(s * 128, (s + 1) * 128)
-            pooled[pair, half_rows, :] = mean
+            pooled[pair, s * 128 : (s + 1) * 128, :] = mean
             normed = act(mean.astype(F32), ones_ref[0:128, 0:128], gain_coarse)
             a2[pair + 1, s * 128 + B : (s + 1) * 128 + B, :] = normed
 
-    fine_pair(0)
-    fine_pair(H - 1)
+    def nth(i):
+        return jnp.where(i == 0, 0, jnp.where(i == 1, H - 1, i - 1))
+
+    def fine_step(q, _):
+        fine_conv(nth(2 * q), g0)
+        fine_post(nth(jnp.maximum(2 * q - 1, 0)), g1)
+        fine_conv(nth(2 * q + 1), g1)
+        fine_post(nth(2 * q), g0)
+        return 0
+
+    g1[...] = jnp.zeros((512, 256), F32)
+    lax.fori_loop(0, 2, fine_step, 0)
+    edges[0] = a2[1, B : B + 256, :]
+    edges[1] = a2[H, B : B + 256, :]
     c_west = pltpu.make_async_remote_copy(
-        src_ref=a2.at[1, pl.ds(B, 256)],
+        src_ref=edges.at[0],
         dst_ref=halo2.at[0],
         send_sem=c_send.at[0],
         recv_sem=c_recv.at[0],
@@ -289,7 +304,7 @@
         device_id_type=MESH,
     )
     c_east = pltpu.make_async_remote_copy(
-        src_ref=a2.at[H, pl.ds(B, 256)],
+        src_ref=edges.at[1],
         dst_ref=halo2.at[1],
         send_sem=c_send.at[1],
         recv_sem=c_recv.at[1],
@@ -299,32 +314,28 @@
     c_west.start()
     c_east.start()
 
-    def fine_loop(pair, _):
-        fine_pair(pair)
-        return 0
-
-    lax.fori_loop(1, H - 1, fine_loop, 0)
-
-    seam_perm(perm_c, seam_ref, 0, H, False)
-    north_south(a2, perm_c, H, H, 0)
-    seam_perm(perm_c, seam_ref, 2, H, False)
-    north_south(a2, perm_c, H, 1, H + 1)
+    lax.fori_loop(2, 8, fine_step, 0)
+    fine_post(H - 2, g1)
+
+    north_south(a2, 0, H, H, 0)
+    north_south(a2, 2, H, 1, H + 1)
     c_west.wait()
     c_east.wait()
-    seam_perm(perm_c, seam_ref, 1, H, False)
-    a2[H + 1, B : B + 256, :] = dot(perm_c[...], halo2[0]).astype(BF16)
-    seam_perm(perm_c, seam_ref, 3, H, False)
-    a2[0, B : B + 256, :] = dot(perm_c[...], halo2[1]).astype(BF16)
-
-    def coarse_loop(pair, _):
-        got = conv_pair(a2, coarse_w[...], pair, 0, 256)
-        base = jnp.concatenate([pooled[2 * pair], pooled[2 * pair + 1]], axis=1)
-        out = (base.astype(F32) + got).astype(BF16)
-        coarse[2 * pair] = out[:, :128]
-        coarse[2 * pair + 1] = out[:, 128:]
+    for side, got, column in ((1, 0, H + 1), (3, 1, 0)):
+        moved = from_side(seam_w[side], halo2[got], H, flipped[side])
+        for r in range(H):
+            a2[column, (r + 1) * B : (r + 2) * B, :] = moved[r].astype(BF16)
+
+    def coarse_loop(q, _):
+        for pair in (2 * q, 2 * q + 1):
+            got = conv_pair(a2, coarse_w[...], pair, 0, 256)
+            base = jnp.concatenate([pooled[2 * pair], pooled[2 * pair + 1]], axis=1)
+            out = (base.astype(F32) + got).astype(BF16)
+            coarse[2 * pair] = out[:, :128]
+            coarse[2 * pair + 1] = out[:, 128:]
         return 0
 
-    lax.fori_loop(0, H // 2, coarse_loop, 0)
+    lax.fori_loop(0, H // 4, coarse_loop, 0)
 
     i, j = iota((512, 128), 0), iota((512, 128), 1)
     slot_ref[...] = jnp.where(
@@ -381,23 +392,17 @@
     def last_stage(k):
         start = k * rows_c
 
-        def pair_step(q, sums):
-            out = []
-            for half in range(2):
-                pair = half * 8 + q
-                f = jnp.concatenate(
-                    [fine[2 * pair, start : start + rows_c, :], fine[2 * pair + 1, start : start + rows_c, :]],
-                    axis=1,
-                ).astype(F32)
-                c = coarse[pair, start // 2 : (start + rows_c) // 2, :].astype(F32)
-                c = c.reshape(RC // 2, 1, B, 128)
-                c = jnp.concatenate([c, c], axis=1).reshape(rows_c, 128)
-                normed = act(f + twice(c), ones_ref[...], gain_out)
-                out.append(sums[half] + dot(normed, out_w[q]))
-            return tuple(out)
-
-        zero = jnp.zeros((rows_c, 128), F32)
-        left, right = lax.fori_loop(0, 8, pair_step, (zero, zero))
+        for pair in range(H):
+            f = jnp.concatenate(
+                [fine[2 * pair, start : start + rows_c, :], fine[2 * pair + 1, start : start + rows_c, :]],
+                axis=1,
+            ).astype(F32)
+            c = coarse[pair, start // 2 : (start + rows_c) // 2, :].astype(F32)
+            c = c.reshape(RC // 2, 1, B, 128)
+            c = jnp.concatenate([c, c], axis=1).reshape(rows_c, 128)
+            act_s[:, pair * 256 : (pair + 1) * 256] = act(f + twice(c), ones_ref[...], gain_out)
+        left = dot(act_s[:, :2048], out_w[...])
+        right = dot(act_s[:, 2048:], out_w[...])
         proj = jnp.concatenate([left, right], axis=1).reshape(RC, B, 256)
         state = nx[start : start + rows_c, :].astype(F32).reshape(RC, B, 256)
         den = (c_skip * state + c_out * proj).reshape(rows_c, 256)
@@ -532,13 +537,12 @@
             pltpu.VMEM((512, 256), BF16),
             pltpu.VMEM((512, 256), BF16),
             pltpu.VMEM((8, 128, 256), BF16),
-            pltpu.VMEM((8, 256, 128), BF16),
+            pltpu.VMEM((2048, 128), BF16),
             pltpu.VMEM((1536, 256), BF16),
             pltpu.VMEM((1536, 256), BF16),
             pltpu.VMEM((256, 256), BF16),
             pltpu.VMEM((512, 512), BF16),
-            pltpu.VMEM((512, 512), BF16),
-            pltpu.VMEM((256, 256), BF16),
+            pltpu.VMEM((4, 256, 256), BF16),
             pltpu.VMEM((512, 128), BF16),
             pltpu.VMEM((64, 512), BF16),
             pltpu.VMEM((2, 512, 128), BF16),
@@ -549,6 +553,10 @@
             pltpu.VMEM((H + 2, 288, 128), BF16),
             pltpu.VMEM((2, 256, 128), BF16),
             pltpu.VMEM((H, 256, 128), BF16),
+            pltpu.VMEM((512, 256), F32),
+            pltpu.VMEM((512, 256), F32),
+            pltpu.VMEM((RC * B, 4096), BF16),
+            pltpu.VMEM((2, 256, 128), BF16),
             pltpu.VMEM(((N + 1) * B, 256), F32),
             pltpu.VMEM((CH, NT, 32, 256), BF16),
             pltpu.VMEM((CH, NT, 32, 256), BF16),
@@ -567,7 +575,7 @@
             dma((CH, NM)),
         ],
         compiler_params=pltpu.CompilerParams(
-            collective_id=0, has_side_effects=True, vmem_limit_bytes=56 * 1024 * 1024
+            collective_id=0, has_side_effects=True, vmem_limit_bytes=36 * 1024 * 1024
         ),
     )(
         noisy.reshape(512, 256),

time: 119 us -> 73.4 us (0.62)
  Pallas kernels: 104 us -> 58 us
  other arithmetic: 2.51 us -> 3.99 us
    pallas_call x1, Pallas kernels: 104 us -> 58 us  [on_device(): pl.pallas_call(kernel, out_shape=(jax.ShapeDtypeStruct((512, 256), F32),...]
    unnamed x31 -> x21, local copies, waits for them, and re-layouts: 4.15 us -> 4.75 us
where the time goes in v2:
time: 73.4 us; the launch traced here: 73.1 us
  Pallas kernels  58 us (79%)
  local copies, waits for them, and re-layouts  10.2 us (14%)
  other arithmetic  3.99 us (5%)
    pallas_call x1, Pallas kernels, on_device(): pl.pallas_call(kernel, out_shape=(jax.ShapeDtypeStruct((512, 256), F32),...  58 us
    unnamed x21, local copies, waits for them, and re-layouts  4.75 us

profile of v2, /device:TPU:1, one launch (start us, length us, event | category | flops | bytes accessed | tf_op | source)
XLA Modules:
  0.0 73.1 jit_solution(1781657213594104521)
XLA Ops:
  0.7 0.5 broadcast.182
  1.2 1.3 %reduce.5 = s32[128]{0:T(128)S(1)} reduce(s32[128,1]{0,1:T(1,128)} %param.18, s32[]{:T(128)} %broadcast.182), dimensions={1}, to_apply=%param.18.reduce_sub_computation.3 | reduce | bytes 1028 | tf_op args[4]
  2.5 0.7 convert_element_type.7
  3.2 0.1 multiply_sine_fusion
  3.3 0.2 divide_multiply_fusion
  3.5 0.8 %slice_bitcast_fusion.2 = (f32[8]{0:T(128)S(1)}, f32[8]{0:T(128)S(1)}) fusion(f32[8,2]{0,1:T(2,128)} %param.20), kind=kLoop, calls=%fused_computation.50 | loop fusion | bytes 128 | tf_op jit(solution)/shard_map/squeeze | solution.py:506
  4.4 0.7 fusion.17
  5.5 0.7 pad_maximum_fusion.gain_ref
  6.5 0.1 convert_reduce_fusion
  6.6 0.2 fusion.4
  6.8 0.1 broadcast_in_dim_tile.3.key_ref
  6.9 0.7 %broadcast_in_dim.53 = s32[16,8]{1,0:T(8,128)S(1)} reshape(s32[128]{0:T(128)} %param.19) | data formatting | bytes 1024 | tf_op jit(solution)/shard_map/jit(_where)/broadcast_in_dim | solution.py:522
  7.8 0.6 gather_fusion
  8.5 0.1 select_n.66
  8.7 0.6 copy-done.5
  9.3 0.1 copy.57
  9.5 0.7 copy-done.6
  10.2 0.1 copy.53.wo_ref
  10.7 0.6 copy-done.4
  11.3 1.0 %copy-done.2 = bf16[9,128,128]{2,1,0:T(8,128)(2,1)S(1)} copy-done((bf16[9,128,128]{2,1,0:T(8,128)(2,1)S(1)}, bf16[9,128,128]{2,1,0:T(8,128)(2,1)}, u32[]{:S(2)}) %copy-start.2) | copy-done | bytes 294936
  12.3 0.9 %copy-done.3 = bf16[2,8,32,256]{3,2,1,0:T(8,128)(2,1)S(1)} copy-done((bf16[2,8,32,256]{3,2,1,0:T(8,128)(2,1)S(1)}, bf16[2,8,32,256]{3,2,1,0:T(8,128)(2,1)}, u32[]{:S(2)}) %copy-start.3) | copy-done | bytes 262168
  13.2 58.0 %shard_map.157 = (f32[512,256]{1,0:T(8,128)S(1)}, f32[4,8,8,256]{3,2,1,0:T(8,128)S(1)}) custom-call(bf16[512,256]{1,0:T(8,128)(2,1)S(1)} %bitcast.28, f32[6,16,128]{2,1,0:T(8,128)S(1)} %constant_dynamic-update-slice_fusion.vec_ref, f32[3,128]{1,0:T(4,128)S(1)} %pad_maximum_fusion.gain_ref, s32[16,12]{1,0:T(8,128)S(1)} %pad_add_fusion.seam_ref, ...), custom_call_target="tpu_custom_call" | custom-call | tf_op jit(solution)/shard_map/pallas_call | solution.py:528
  71.2 1.1 %copy.54 = f32[16,32,256]{2,1,0:T(8,128)} copy(f32[16,32,256]{2,0,1:T(8,128)S(1)} %bitcast.27) | data formatting | bytes 1048576 | tf_op jit(solution)/shard_map/transpose | solution.py:592
  72.4 0.7 slice_bitcast_fusion
  (42 shorter events, 1.8 us)
Async XLA Ops:
  0.6 2.7 %copy-start = (f32[128,128]{1,0:T(8,128)S(1)}, f32[128,128]{1,0:T(8,128)}, u32[]{:S(2)}) copy-start(f32[128,128]{1,0:T(8,128)} %param.21) | copy-start | bytes 196612
  0.6 10.0 %copy-start.1 = (bf16[9,128,128]{2,1,0:T(8,128)(2,1)S(1)}, bf16[9,128,128]{2,1,0:T(8,128)(2,1)}, u32[]{:S(2)}) copy-start(bf16[9,128,128]{2,1,0:T(8,128)(2,1)} %wf_ref.1) | copy-start | bytes 884740
  8.6 0.7 copy-start.5
  9.5 0.7 copy-start.6
  10.6 0.7 copy-start.4
  11.3 1.0 %copy-start.2 = (bf16[9,128,128]{2,1,0:T(8,128)(2,1)S(1)}, bf16[9,128,128]{2,1,0:T(8,128)(2,1)}, u32[]{:S(2)}) copy-start(bf16[9,128,128]{2,1,0:T(8,128)(2,1)} %wc_ref.1) | copy-start | bytes 884740
  12.3 0.9 %copy-start.3 = (bf16[2,8,32,256]{3,2,1,0:T(8,128)(2,1)S(1)}, bf16[2,8,32,256]{3,2,1,0:T(8,128)(2,1)}, u32[]{:S(2)}) copy-start(bf16[2,8,32,256]{3,2,1,0:T(8,128)(2,1)} %param.15) | copy-start | bytes 786436

commit v3 on v0

v3 whole, which is shorter than its diff:
```python
import functools
import math

import jax
import jax.numpy as jnp
from jax import lax
from jax.experimental import pallas as pl
from jax.experimental.pallas import tpu as pltpu
from jax.sharding import PartitionSpec as P

STEPS = 1000
MESH = pl.DeviceIdType.MESH
F32 = jnp.float32
BF16 = jnp.bfloat16

B = 16
N = 32
H = N // 2
NT = 16
NM = 8
DUMMY = H + 1
FIRST = 10
EARLY = 4
CHUNK = 128


def dot(a, b):
    return jnp.dot(a, b, preferred_element_type=F32)


def twice(x):
    return jnp.concatenate([x, x], axis=-1)


def iota(shape, dim):
    return lax.broadcasted_iota(jnp.int32, shape, dim)


def onehot(where):
    return jnp.where(where, 1.0, 0.0).astype(BF16)


def act(x, ones, half_gain):
    mean = dot((x * x).astype(BF16), ones)
    h = x * lax.rsqrt(mean + 1e-06) * half_gain
    return (h + h * jnp.tanh(h)).astype(BF16)


def column(row):
    spread = jnp.broadcast_to(row.astype(F32), (B, 8))
    own = iota((B, 8), 1) == (iota((B, 8), 0) & 7)
    return jnp.sum(jnp.where(own, spread, 0.0), axis=1, keepdims=True)


def from_side(perm, edge, n, flipped):
    rows = edge.shape[0]
    if rows > 256:
        edge = jnp.concatenate([edge[:256], edge[256:]], axis=1)
        got = dot(perm[...], edge)
        pieces = [
            got[c % H * B : (c % H + 1) * B, c // H * 128 : (c // H + 1) * 128] for c in range(n)
        ]
    else:
        got = dot(perm[:rows, :rows], edge)
        pieces = [got[c * B : (c + 1) * B] for c in range(n)]
    if edge.shape[1] > 128 and rows <= 256:
        flipped = twice(flipped)
    return [
        jnp.where(flipped > 0.5, pieces[n - 1 - c], pieces[c]) for c in range(n)
    ]


def conv_weights(out_ref, w_ref):
    zero = jnp.zeros((128, 128), BF16)
    for i in range(3):
        for j in range(4):
            left = w_ref[3 * i + j] if j < 3 else zero
            right = w_ref[3 * i + j - 1] if j > 0 else zero
            start = (4 * i + j) * 128
            out_ref[start : start + 128, :] = jnp.concatenate([left, right], axis=1)


def conv_pair(a_ref, w_ref, pair, rows):
    parts = []
    for i in range(3):
        for j in range(4):
            parts.append(a_ref[2 * pair + j, i * B : i * B + rows, :])
    return dot(jnp.concatenate(parts, axis=1), w_ref[...])


def each(count, what):
    def body(d, _):
        what(d)
        return 0

    lax.fori_loop(1, count, body, 0)


def kernel(
    noisy_ref,
    step_ref,
    seam_ref,
    route_ref,
    block_ref,
    frac_ref,
    wt_ref,
    wl_ref,
    wf_hbm,
    wc_hbm,
    gf_ref,
    gc_ref,
    go_ref,
    wo_ref,
    den_ref,
    stat_ref,
    wf_ref,
    wc_ref,
    nx,
    sx,
    lift_w,
    out_w,
    fine_w,
    coarse_w,
    ones_ref,
    seam_w,
    slot_ref,
    sum_ref,
    halo,
    started0,
    started1,
    a10,
    a11,
    fine0,
    fine1,
    pooled0,
    pooled1,
    a20,
    a21,
    coarse0,
    coarse1,
    halo2,
    edges,
    g0,
    g1,
    act_s,
    d_ref,
    send,
    recv,
    tgt,
    mrecv,
    gat,
    w_sem,
    h_send,
    h_recv,
    c_send,
    c_recv,
    a_send,
    a_recv,
    m_send,
    m_recv,
    g_send,
    g_recv,
):
    pos = lax.axis_index("tile")
    mem = lax.axis_index("mem")
    started, a1, fine = (started0, started1), (a10, a11), (fine0, fine1)
    pooled, a2, coarse = (pooled0, pooled1), (a20, a21), (coarse0, coarse1)

    def along_tile(d):
        return {"tile": lax.rem(pos + d, NT)}

    def along_mem(d):
        return {"mem": lax.rem(mem + d, NM)}

    barrier = pltpu.get_barrier_semaphore()

    def greet(where):
        pl.semaphore_signal(barrier, inc=1, device_id=where, device_id_type=MESH)

    each(NT, lambda d: greet(along_tile(d)))
    each(NM, lambda d: greet(along_mem(d)))

    load_fine = pltpu.make_async_copy(wf_hbm, wf_ref, w_sem.at[0])
    load_coarse = pltpu.make_async_copy(wc_hbm, wc_ref, w_sem.at[1])
    load_fine.start()
    load_coarse.start()

    ones_ref[...] = jnp.where(
        iota((256, 256), 0) // 128 == iota((256, 256), 1) // 128, 1.0 / 128, 0.0
    ).astype(BF16)
    wl = wl_ref[...].astype(F32)
    wl_zero = jnp.zeros_like(wl)
    wl_pair = jnp.concatenate(
        [
            jnp.concatenate([wl, wl_zero], axis=1),
            jnp.concatenate([wl_zero, wl], axis=1),
        ],
        axis=0,
    ).astype(BF16)
    for q in range(8):
        lift_w[q] = jnp.zeros((128, 256), BF16)
        lift_w[q, q * B : (q + 1) * B, :] = wl_pair

    level = jnp.where(iota((8, 128), 0) < 4, step_ref[0], step_ref[1]).astype(F32)
    fraction = level / (STEPS - 1)
    high_root = 80.0 ** (1.0 / 7.0)
    low_root = 0.002 ** (1.0 / 7.0)
    root = high_root + fraction * (low_root - high_root)
    square = root * root
    sigma = square * square * square * root
    denominator = sigma * sigma + 1.0
    scales = (lax.rsqrt(denominator), 1.0 / denominator, sigma * lax.rsqrt(denominator))
    c_in, c_skip, c_out = [[twice(x[0:1]), twice(x[4:5])] for x in scales]
    lane = iota((8, 128), 1)
    frequency = jnp.exp((lane & 63).astype(F32) * (-math.log(10000.0) / 64))
    angles = level * frequency
    features = jnp.where(lane < 64, jnp.sin(angles), jnp.cos(angles))
    embedded = jnp.dot(
        features, wt_ref[...], preferred_element_type=F32, precision=lax.Precision.HIGHEST
    )
    embedded = embedded / (1.0 + jnp.exp(-embedded))
    temb = [twice(embedded[0:1]), twice(embedded[4:5])]
    gain_fine = twice(gf_ref[...]) * 0.5
    gain_coarse = gc_ref[...] * 0.5
    gain_out = twice(go_ref[...]) * 0.5

    i = iota((256, 256), 0)
    to_rows = onehot(((i & 7) * N + ((i >> 3) & 1) * H + (i >> 4)) == iota((256, 256), 1))
    for m in range(2):
        moved = dot(to_rows, noisy_ref[m * 256 : (m + 1) * 256, :])
        nx[m * 256 : (m + 1) * 256, :] = moved.astype(BF16)
        sx[m * 256 : (m + 1) * 256, :] = (moved * c_in[m]).astype(BF16)

    def lift(m):
        def body(step, _):
            for q in (2 * step, 2 * step + 1):
                for half in range(2):
                    pair = half * 8 + q
                    cells = sx[m * 256 : (m + 1) * 256, half * 128 : (half + 1) * 128]
                    first = (dot(cells, lift_w[q]) + temb[m]).astype(BF16)
                    started[m][2 * pair] = first[:, :128]
                    started[m][2 * pair + 1] = first[:, 128:]
                    normed = act(first.astype(F32), ones_ref[...], gain_fine)
                    a1[m][2 * pair + 1, B : B + 256, :] = normed[:, :128]
                    a1[m][2 * pair + 2, B : B + 256, :] = normed[:, 128:]
            return 0

        lax.fori_loop(0, 4, body, 0)

    lift(0)

    half = iota((B, 1), 0) >> 3
    own = iota((B, 1), 0) & 7
    flipped = []
    for side in range(4):
        tile = column(seam_ref[0, side : side + 1, :] & 7).astype(jnp.int32)
        flag = column(seam_ref[2, side : side + 1, :]).astype(jnp.int32)
        if side == 0:
            source = jnp.where(half == 0, 8 + tile, own)
            flag = jnp.where(half == 0, flag, 0)
        elif side == 2:
            source = jnp.where(half == 0, 8 + own, tile)
            flag = jnp.where(half == 0, 0, flag)
        else:
            source = ((half + flag) & 1) * 8 + tile
        flipped.append(jnp.broadcast_to(flag.astype(F32), (B, 128)))
        apart = iota((B, 256), 1) - source
        for c in range(256 // B):
            seam_w[side, c * B : (c + 1) * B, :] = onehot(apart == c * B)

    def north_south(a_ref, cols, rows):
        for side, row_from, row_to in ((0, rows, 0), (2, 1, rows + 1)):
            edge = a_ref[1 : cols + 1, row_from * B : (row_from + 1) * B, :]
            got = from_side(seam_w.at[side], edge.reshape(cols * B, 128), cols, flipped[side])
            for c in range(cols):
                a_ref[c + 1, row_to * B : (row_to + 1) * B, :] = got[c].astype(BF16)

    def corners(a_ref, cols, rows):
        for col, inner in ((0, 1), (cols + 1, cols)):
            north = a_ref[inner, 0:B, :].astype(F32)
            south = a_ref[inner, (rows + 1) * B : (rows + 2) * B, :].astype(F32)
            last = a_ref[col, rows * B : (rows + 1) * B, :].astype(F32)
            first = a_ref[col, B : 2 * B, :].astype(F32)
            a_ref[col, 0:B, :] = jnp.concatenate([north[:8], last[:8]], axis=0).astype(BF16)
            a_ref[col, (rows + 1) * B : (rows + 2) * B, :] = jnp.concatenate(
                [first[8:], south[8:]], axis=0
            ).astype(BF16)

    north_south(a10, N, H)
    load_fine.wait()
    conv_weights(fine_w, wf_ref)
    lift(1)

    pl.semaphore_wait(barrier, NT - 1 + NM - 1)

    def h_copy(side):
        return pltpu.make_async_remote_copy(
            src_ref=nx.at[:, pl.ds(side * 128, 128)],
            dst_ref=halo.at[side],
            send_sem=h_send.at[side],
            recv_sem=h_recv.at[side],
            device_id=along_tile(1 if side else NT - 1),
            device_id_type=MESH,
        )

    def c_copy(m, side):
        return pltpu.make_async_remote_copy(
            src_ref=edges.at[m, side],
            dst_ref=halo2.at[m, side],
            send_sem=c_send.at[m, side],
            recv_sem=c_recv.at[m, side],
            device_id=along_tile(1 if side else NT - 1),
            device_id_type=MESH,
        )

    for side in range(2):
        h_copy(side).start()

    def fine_post(m, pair, buf):
        base = jnp.concatenate([started[m][2 * pair], started[m][2 * pair + 1]], axis=1)
        out = (base.astype(F32) + buf[...]).astype(BF16)
        fine[m][2 * pair] = out[:, :128]
        fine[m][2 * pair + 1] = out[:, 128:]
        wide = out.astype(F32).reshape(H // 2, 2, B, 256)
        tall = wide[:, 0] + wide[:, 1]
        mean = ((tall[:, :, :128] + tall[:, :, 128:]) * 0.25).reshape(128, 128).astype(BF16)
        pooled[m][pair] = mean
        a2[m][pair + 1, B : B + 128, :] = act(mean.astype(F32), ones_ref[0:128, 0:128], gain_coarse)

    def fine_pairs(m, count, nth):
        def body(q, _):
            g0[...] = conv_pair(a1[m], fine_w, nth(2 * q), 256)
            fine_post(m, jnp.where(q == 0, DUMMY, nth(2 * q - 1)), g1)
            g1[...] = conv_pair(a1[m], fine_w, nth(2 * q + 1), 256)
            fine_post(m, nth(2 * q), g0)
            return 0

        lax.fori_loop(0, count // 2, body, 0)
        fine_post(m, nth(count - 1), g1)

    def ends(i):
        return i * (H - 1)

    def send_edges(m):
        edges[m, 0] = a2[m][1, B : B + 128, :]
        edges[m, 1] = a2[m][H, B : B + 128, :]
        for side in range(2):
            c_copy(m, side).start()

    g1[...] = jnp.zeros((256, 256), F32)
    fine_pairs(0, H - 2, lambda i: i + 1)

    north_south(a11, N, H)
    for side in range(2):
        h_copy(side).wait()
    sides = []
    for side, got, w in ((3, 1, lift_w[7, :, 128:256]), (1, 0, lift_w[0, :, 0:128])):
        both = jnp.concatenate([halo[got, 0:256, :], halo[got, 256:512, :]], axis=1)
        moved = jnp.concatenate(from_side(seam_w.at[side], both, H, flipped[side]), axis=0)
        sides.append(
            [
                dot((moved[:, m * 128 : (m + 1) * 128] * c_in[m][:, :128]).astype(BF16), w)
                for m in range(2)
            ]
        )
    for m in range(2):
        first = (jnp.concatenate([sides[0][m], sides[1][m]], axis=1) + temb[m]).astype(BF16)
        normed = act(first.astype(F32), ones_ref[...], gain_fine)
        a1[m][0, B : B + 256, :] = normed[:, :128]
        a1[m][N + 1, B : B + 256, :] = normed[:, 128:]
        corners(a1[m], N, H)

    fine_pairs(0, 2, ends)
    send_edges(0)
    fine_pairs(1, 2, ends)
    send_edges(1)
    load_coarse.wait()
    conv_weights(coarse_w, wc_ref)
    for q in range(8):
        for j in range(2):
            place = onehot(iota((8, 128), 1) == iota((8, 128), 0) + (16 * q + 8 * j))
            out_w[(2 * q + j) * 128 : (2 * q + j + 1) * 128, :] = lax.dot_general(
                wo_ref[...], place, (((0,), (0,)), ((), ())), preferred_element_type=F32
            ).astype(BF16)
    frac_p, frac_q = [
        jnp.broadcast_to(column(frac_ref[k : k + 1, :]), (B, 256)) for k in range(2)
    ]

    route = jnp.broadcast_to(route_ref[...], (8, 128))
    rank = jnp.zeros((8, 128), jnp.int32)
    for s in range(1, 8):
        again = (pltpu.roll(route, s, 1) == route) & ((lane & 7) >= s)
        rank = rank + jnp.where(again, 1, 0)
    key = ((route - pos) & (NT - 1)) * 2 + rank
    pick = onehot(iota((128, 128), 0) == pos * 8 + (iota((128, 128), 1) & 7))
    key = dot(key.astype(F32).astype(BF16), pick)[0:1, :]
    i, j = iota((512, 128), 0), iota((512, 128), 1)
    slot_ref[...] = onehot(
        ((i >> 4).astype(F32) == key) & (((i >> 3) & 1) == ((j >> 3) & 1)) & ((i & 7) == (j >> 4))
    )
    slot = jnp.where(route == pos, ((pos - (lane >> 3)) & (NT - 1)) * 2 + rank, -1).astype(F32)
    diagonal = iota((128, 128), 0) == iota((128, 128), 1)
    slot = jnp.sum(jnp.where(diagonal, slot[0:1, :], 0.0), axis=1, keepdims=True)
    pick = onehot(slot == (iota((128, 512), 1) >> 4).astype(F32))
    block = jnp.broadcast_to(block_ref[...], (8, 128)).astype(F32) + 1.0
    block = dot(block.astype(BF16), pick)[0:1, :]
    i, j = iota((64, 512), 0), iota((64, 512), 1)
    sum_ref[...] = onehot(
        (((i & 3) + 1).astype(F32) == block)
        & (((i >> 2) & 1) == ((j >> 3) & 1))
        & ((i >> 3) == (j & 7))
    )

    def a_copy(k, d):
        return pltpu.make_async_remote_copy(
            src_ref=send.at[k, d],
            dst_ref=recv.at[k, d],
            send_sem=a_send.at[k, d],
            recv_sem=a_recv.at[k, d],
            device_id=along_tile(d),
            device_id_type=MESH,
        )

    def m_copy(m, d):
        return pltpu.make_async_remote_copy(
            src_ref=tgt.at[m, lax.rem(mem + d, NM)],
            dst_ref=mrecv.at[m, d],
            send_sem=m_send.at[m, d],
            recv_sem=m_recv.at[m, d],
            device_id=along_mem(d),
            device_id_type=MESH,
        )

    def g_copy(d):
        return pltpu.make_async_remote_copy(
            src_ref=gat.at[mem],
            dst_ref=gat.at[mem],
            send_sem=g_send.at[d],
            recv_sem=g_recv.at[d],
            device_id=along_mem(d),
            device_id_type=MESH,
        )

    def coarse_level(m):
        north_south(a2[m], H, H // 2)
        for side in range(2):
            c_copy(m, side).wait()
        for side, got, col in ((1, 0, H + 1), (3, 1, 0)):
            moved = from_side(seam_w.at[side], halo2[m, got], H // 2, flipped[side])
            for r in range(H // 2):
                a2[m][col, (r + 1) * B : (r + 2) * B, :] = moved[r].astype(BF16)
        corners(a2[m], H, H // 2)

        def body(q, _):
            for pair in (4 * q, 4 * q + 1, 4 * q + 2, 4 * q + 3):
                got = conv_pair(a2[m], coarse_w, pair, 128)
                base = jnp.concatenate([pooled[m][2 * pair], pooled[m][2 * pair + 1]], axis=1)
                out = (base.astype(F32) + got).astype(BF16)
                coarse[m][2 * pair] = out[:, :128]
                coarse[m][2 * pair + 1] = out[:, 128:]
            return 0

        lax.fori_loop(0, 2, body, 0)

    def state(m, row, count):
        start, rows = row * B, count * B
        for pair in range(H):
            f = jnp.concatenate(
                [
                    fine[m][2 * pair, start : start + rows, :],
                    fine[m][2 * pair + 1, start : start + rows, :],
                ],
                axis=1,
            ).astype(F32)
            c = coarse[m][pair, start // 2 : (start + rows) // 2, :].astype(F32)
            c = c.reshape(count // 2, 1, B, 128)
            c = jnp.concatenate([c, c], axis=1).reshape(rows, 128)
            act_s[:rows, pair * 256 : (pair + 1) * 256] = act(f + twice(c), ones_ref[...], gain_out)
        left = dot(act_s[:rows, :2048], out_w[...])
        right = dot(act_s[:rows, 2048:], out_w[...])
        proj = jnp.concatenate([left, right], axis=1)
        cells = slice(m * 256 + start, m * 256 + start + rows)
        den = c_skip[m] * nx[cells, :].astype(F32) + c_out[m] * proj
        d_ref[start : start + rows, :] = den
        den_ref[cells, :] = den

    def route_rows(m, k):
        start = k * CHUNK
        den = d_ref[start : start + CHUNK, :].reshape(8, B, 256)
        below = d_ref[start + B : start + B + CHUNK, :].reshape(8, B, 256)
        mixed = ((1.0 - frac_p) * den + frac_p * below).reshape(CHUNK, 256)
        shifted = pltpu.roll(mixed, 248, 1)
        shifted = jnp.where(iota((CHUNK, 256), 1) >= 248, mixed, shifted)
        out = (1.0 - frac_q) * mixed.reshape(8, B, 256) + frac_q * shifted.reshape(8, B, 256)
        blocks = dot(slot_ref[...], out.reshape(CHUNK, 256).astype(BF16)).astype(BF16)
        blocks = blocks.reshape(NT, 32, 256)
        recv[2 * m + k, 0] = blocks[0]
        send[2 * m + k] = blocks
        each(NT, lambda d: a_copy(2 * m + k, d).start())

    def last_stage(m):
        state(m, 0, FIRST)
        route_rows(m, 0)
        state(m, FIRST, H - FIRST)
        d_ref[H * B :, :] = jnp.concatenate([d_ref[8:16, :], d_ref[H * B - 8 : H * B, :]], axis=0)
        route_rows(m, 1)

    def sum_stage(m):
        for k in range(2):
            each(NT, lambda d: a_copy(2 * m + k, d).wait_recv())
            total = dot(sum_ref[...], recv[2 * m + k].reshape(512, 256))
            tgt[m, :, k] = total.reshape(NM, 8, 256)
        mrecv[m, 0] = tgt[m, mem]
        each(NM, lambda d: m_copy(m, d).start())

    fine_pairs(1, EARLY, lambda i: i + 1)
    coarse_level(0)
    last_stage(0)
    fine_pairs(1, H - 2 - EARLY, lambda i: i + 1 + EARLY)
    coarse_level(1)
    last_stage(1)
    sum_stage(0)
    sum_stage(1)

    for m in range(2):
        each(NM, lambda d: m_copy(m, d).wait_recv())
    total = jnp.zeros((2, 8, 256), F32)
    for m in range(2):
        for d in range(NM):
            total = total + mrecv[m, d]
    mean = total * (1.0 / 16)
    squares = jnp.zeros((2, 8, 256), F32)
    for m in range(2):
        for d in range(NM):
            dev = mrecv[m, d] - mean
            squares = squares + dev * dev
    gat[mem, 0] = mean
    gat[mem, 1] = jnp.sqrt(squares / 15.0 + 1e-06)
    each(NM, lambda d: g_copy(d).start())
    each(NM, lambda d: g_copy(d).wait_recv())
    stat_ref[...] = gat[...]
    for k in range(4):
        each(NT, lambda d: a_copy(k, d).wait_send())
    for m in range(2):
        each(NM, lambda d: m_copy(m, d).wait_send())
    each(NM, lambda d: g_copy(d).wait_send())


def on_device(
    noisy,
    timestep,
    seams,
    corner_list,
    route,
    target_block,
    frac,
    w_time,
    w_lift,
    w_fine,
    w_coarse,
    gain_fine,
    gain_coarse,
    gain_out,
    w_out,
):
    vmem = pl.BlockSpec(memory_space=pltpu.VMEM)
    smem = pl.BlockSpec(memory_space=pltpu.SMEM)
    hbm = pl.BlockSpec(memory_space=pltpu.HBM)
    dma = pltpu.SemaphoreType.DMA
    den, stat = pl.pallas_call(
        kernel,
        out_shape=(
            jax.ShapeDtypeStruct((512, 256), F32),
            jax.ShapeDtypeStruct((NM, 2, 2, 8, 256), F32),
        ),
        in_specs=[vmem, smem] + [vmem] * 6 + [hbm] * 2 + [vmem] * 4,
        out_specs=(vmem, vmem),
        scratch_shapes=[
            pltpu.VMEM((9, 128, 128), BF16),
            pltpu.VMEM((9, 128, 128), BF16),
            pltpu.VMEM((512, 256), BF16),
            pltpu.VMEM((512, 256), BF16),
            pltpu.VMEM((8, 128, 256), BF16),
            pltpu.VMEM((2048, 128), BF16),
            pltpu.VMEM((1536, 256), BF16),
            pltpu.VMEM((1536, 256), BF16),
            pltpu.VMEM((256, 256), BF16),
            pltpu.VMEM((4, 256, 256), BF16),
            pltpu.VMEM((512, 128), BF16),
            pltpu.VMEM((64, 512), BF16),
            pltpu.VMEM((2, 512, 128), BF16),
        ]
        + [pltpu.VMEM((2 * DUMMY + 2, 256, 128), BF16)] * 2
        + [pltpu.VMEM((N + 2, 288, 128), BF16)] * 2
        + [pltpu.VMEM((2 * DUMMY + 2, 256, 128), BF16)] * 2
        + [pltpu.VMEM((DUMMY + 1, 128, 128), BF16)] * 2
        + [pltpu.VMEM((DUMMY + 2, 160, 128), BF16)] * 2
        + [pltpu.VMEM((H, 128, 128), BF16)] * 2
        + [
            pltpu.VMEM((2, 2, 128, 128), BF16),
            pltpu.VMEM((2, 2, 128, 128), BF16),
            pltpu.VMEM((256, 256), F32),
            pltpu.VMEM((256, 256), F32),
            pltpu.VMEM((FIRST * B, 4096), BF16),
            pltpu.VMEM(((H + 1) * B, 256), F32),
            pltpu.VMEM((4, NT, 32, 256), BF16),
            pltpu.VMEM((4, NT, 32, 256), BF16),
            pltpu.VMEM((2, NM, 2, 8, 256), F32),
            pltpu.VMEM((2, NM, 2, 8, 256), F32),
            pltpu.VMEM((NM, 2, 2, 8, 256), F32),
            dma((2,)),
            dma((2,)),
            dma((2,)),
            dma((2, 2)),
            dma((2, 2)),
            dma((4, NT)),
            dma((4, NT)),
            dma((2, NM)),
            dma((2, NM)),
            dma((NM,)),
            dma((NM,)),
        ],
        compiler_params=pltpu.CompilerParams(
            collective_id=0, has_side_effects=True, vmem_limit_bytes=36 * 1024 * 1024
        ),
    )(
        noisy.reshape(512, 256),
        timestep,
        seams.transpose(2, 1, 0),
        route.reshape(1, 128),
        target_block.reshape(1, 128),
        frac.T,
        w_time,
        w_lift,
        w_fine,
        w_coarse,
        gain_fine.reshape(1, 128),
        gain_coarse.reshape(1, 128),
        gain_out.reshape(1, 128),
        w_out.T,
    )
    denoised = den.reshape(2, H, 2, 8, 256).transpose(0, 3, 2, 1, 4).reshape(noisy.shape)
    stat = stat.reshape(NM, 2, 2, 2, 4, 256).transpose(1, 4, 3, 2, 0, 5).reshape(2, 4, N, 256)
    return (denoised, stat[0], stat[1])


def solution(mesh):
    placed = (
        P("mem", "tile", None, None),
        P("mem"),
        P("tile", None, None),
        P("tile", None, None),
        P(),
        P(),
        P("tile", None),
        P(),
        P(),
        P(),
        P(),
        P(),
        P(),
        P(),
        P(),
    )
    return jax.shard_map(
        on_device,
        mesh=mesh,
        in_specs=placed,
        out_specs=(P("mem", "tile", None, None), P("tile", None, None), P("tile", None, None)),
        check_vma=False,
    )
```

time: 434 us -> 62.7 us (0.14); the launches traced: 428 us -> 62.4 us
  waiting for transfers between devices: 233 us -> 0 us
  other arithmetic: 70.3 us -> 0 us
  Pallas kernels: 0 us -> 54.5 us
  local copies, waits for them, and re-layouts: 60.3 us -> 7.11 us
  matrix products: 36 us -> 0 us
  between operations: 15.5 us -> 0.75 us
  starting transfers between devices: 12.1 us -> 0 us
    psum x2 -> x0, waiting for transfers between devices: 115 us -> none  [the longest x1 58 us: on_device(): summed = lax.psum(jnp.sum(target, axis=0), 'mem')]
    unnamed x4 -> x0, waiting for transfers between devices: 105 us -> none
    pallas_call x0 -> x1, Pallas kernels: none -> 54.5 us  [on_device(): pl.pallas_call(kernel, out_shape=(jax.ShapeDtypeStruct((512, 256), F32),...]
    dot_general x22 -> x0, matrix products: 36 us -> none  [the longest x18 23.8 us: convolve(): jnp.dot(slab_view, weight[3 * row_off + col_off], preferred_element_type=...]
    reduce_sum x5 -> x0, other arithmetic: 25 us -> none  [the longest x2 11.8 us: rms_act(): jnp.mean(values * values, axis=-1, keepdims=True) + 1e-06]
    concatenate x7 -> x0, other arithmetic: 19 us -> none  [the longest x2 10.4 us: assemble(): jnp.concatenate([west_rim[:, :, :, None], normed, east_rim[:, :, :, None]...]
    convert_element_type x6 -> x0, other arithmetic: 15.6 us -> none  [the longest x3 9.33 us: rms_act(): return jax.nn.silu(normed).astype(jnp.bfloat16)]
    slice x15 -> x3, local copies, waits for them, and re-layouts: 15.9 us -> 1.49 us  [on_device(): return (denoised, stat[0], stat[1])]
  transfers between devices with their start and end apart: 7 -> 0, of which waited for: 5 -> 0; matrix products, arithmetic and copies ran while one was open for 1% -> 0% of each run, Pallas kernels for 0% -> 0%
where the time goes in v3:
time: 62.7 us; the launch traced here: 62.4 us
  Pallas kernels  54.5 us (87%)
  local copies, waits for them, and re-layouts  7.11 us (11%)
  between operations  0.75 us (1%)
    pallas_call x1, Pallas kernels, on_device(): pl.pallas_call(kernel, out_shape=(jax.ShapeDtypeStruct((512, 256), F32),...  54.5 us
    unnamed x28, local copies, waits for them, and re-layouts  4.45 us
    slice x3, local copies, waits for them, and re-layouts, on_device(): return (denoised, stat[0], stat[1])  1.49 us

profile of v3, /device:TPU:1, one launch (start us, length us, event | category | flops | bytes accessed | tf_op | source)
XLA Modules:
  0.0 62.4 jit_solution(4033099215776763450)
XLA Ops:
  0.6 0.0 copy-start.12
  0.6 0.0 copy-start.13
  0.7 0.0 copy-start.8
  0.7 0.0 copy-start.9
  0.7 0.0 copy-start.10
  0.7 0.6 copy-done.12
  1.3 0.0 copy-done.13
  1.3 0.0 copy-done.8
  1.3 0.0 copy-done.9
  1.3 0.0 copy-done.10
  1.4 0.0 copy-done.11
  1.4 0.1 copy-done.4
  1.4 0.0 copy-done.6
  1.4 0.0 copy-done.5
  1.4 0.0 copy-done.7
  1.5 1.0 %copy-done = bf16[9,128,128]{2,1,0:T(8,128)(2,1)S(1)} copy-done((bf16[9,128,128]{2,1,0:T(8,128)(2,1)S(1)}, bf16[9,128,128]{2,1,0:T(8,128)(2,1)}, u32[]{:S(2)}) %copy-start) | copy-done | bytes 294936
  2.4 1.0 %copy-done.1 = bf16[9,128,128]{2,1,0:T(8,128)(2,1)S(1)} copy-done((bf16[9,128,128]{2,1,0:T(8,128)(2,1)S(1)}, bf16[9,128,128]{2,1,0:T(8,128)(2,1)}, u32[]{:S(2)}) %copy-start.1) | copy-done | bytes 294936
  3.4 0.9 %copy-done.2 = bf16[2,8,32,256]{3,2,1,0:T(8,128)(2,1)S(1)} copy-done((bf16[2,8,32,256]{3,2,1,0:T(8,128)(2,1)S(1)}, bf16[2,8,32,256]{3,2,1,0:T(8,128)(2,1)}, u32[]{:S(2)}) %copy-start.2) | copy-done | bytes 262168
  4.3 0.8 %copy-done.3 = f32[128,128]{1,0:T(8,128)S(1)} copy-done((f32[128,128]{1,0:T(8,128)S(1)}, f32[128,128]{1,0:T(8,128)}, u32[]{:S(2)}) %copy-start.3) | copy-done | bytes 65560
  5.2 54.5 %shard_map.157 = (f32[512,256]{1,0:T(8,128)S(1)}, f32[8,2,2,8,256]{4,3,2,1,0:T(8,128)S(1)}) custom-call(bf16[512,256]{1,0:T(8,128)(2,1)S(1)} %bitcast.19, s32[2]{0:T(128)S(1)} %copy-done.8, s32[3,4,8]{2,1,0:T(4,128)S(1)} %bitcast.20, s32[1,128]{1,0:T(1,128)S(1)} %bitcast.23, s32[1,128]{1,0:T(1,128)S(1)} %bitcast.24, f32[2,8]{1,0:T(2,128)S(1)} %bitcast.22, ...), custom_call_target="tpu_custom_call" | custom-call | tf_op jit(solution)/shard_map/pallas_call | solution.py:570
  59.7 1.1 %copy.17 = f32[2,8,2,16,256]{4,3,2,1,0:T(8,128)} copy(f32[2,8,2,16,256]{4,1,2,3,0:T(8,128)S(1)} %bitcast.18) | data formatting | bytes 1048576 | tf_op jit(solution)/shard_map/transpose | solution.py:642
  60.8 0.1 reshape.46
  60.9 0.7 %copy.19 = f32[1,4,2,2,8,256]{5,4,3,2,1,0:T(8,128)} copy(f32[1,4,2,2,8,256]{5,1,2,3,0,4:T(4,128)S(1)} %get-tuple-element.7) | data formatting | bytes 262144 | tf_op jit(solution)/shard_map/slice | solution.py:644
  61.6 0.7 %copy.18 = f32[1,4,2,2,8,256]{5,4,3,2,1,0:T(8,128)} copy(f32[1,4,2,2,8,256]{5,1,2,3,0,4:T(4,128)S(1)} %get-tuple-element.8) | data formatting | bytes 262144 | tf_op jit(solution)/shard_map/slice | solution.py:644
  (10 shorter events, 0.0 us)
Async XLA Ops:
  0.6 0.7 %copy-start.12 = (f32[128]{0:T(128)S(1)}, f32[128]{0:T(128)}, u32[]{:S(2)}) copy-start(f32[128]{0:T(128)} %param.26) | copy-start | bytes 1540
  0.6 0.7 %copy-start.13 = (f32[128]{0:T(128)S(1)}, f32[128]{0:T(128)}, u32[]{:S(2)}) copy-start(f32[128]{0:T(128)} %param.27) | copy-start | bytes 1540
  0.7 0.7 %copy-start.8 = (s32[2]{0:T(128)S(1)}, s32[2]{0:T(128)}, u32[]{:S(2)}) copy-start(s32[2]{0:T(128)} %step_ref.1) | copy-start | bytes 28
  0.7 0.7 %copy-start.9 = (s32[128,1]{0,1:T(1,128)S(1)}, s32[128,1]{0,1:T(1,128)}, u32[]{:S(2)}) copy-start(s32[128,1]{0,1:T(1,128)} %param.18) | copy-start | bytes 1540
  0.7 0.7 %copy-start.10 = (s32[128]{0:T(128)S(1)}, s32[128]{0:T(128)}, u32[]{:S(2)}) copy-start(s32[128]{0:T(128)} %param.19) | copy-start | bytes 1540
  0.7 0.7 %copy-start.11 = (f32[128]{0:T(128)S(1)}, f32[128]{0:T(128)}, u32[]{:S(2)}) copy-start(f32[128]{0:T(128)} %param.25) | copy-start | bytes 1540
  0.7 0.7 %copy-start.4 = (s32[8,4,3]{0,1,2:T(4,128)S(1)}, s32[8,4,3]{0,1,2:T(4,128)}, u32[]{:S(2)}) copy-start(s32[8,4,3]{0,1,2:T(4,128)} %param.17) | copy-start | bytes 1156
  0.7 0.7 %copy-start.6 = (bf16[128,8]{0,1:T(8,128)(2,1)S(1)}, bf16[128,8]{0,1:T(8,128)(2,1)}, u32[]{:S(2)}) copy-start(bf16[128,8]{0,1:T(8,128)(2,1)} %param.28) | copy-start | bytes 6148
  0.7 0.7 %copy-start.5 = (bf16[8,128]{1,0:T(8,128)(2,1)S(1)}, bf16[8,128]{1,0:T(8,128)(2,1)}, u32[]{:S(2)}) copy-start(bf16[8,128]{1,0:T(8,128)(2,1)} %wl_ref.1) | copy-start | bytes 6148
  0.7 0.7 %copy-start.7 = (f32[8,2]{0,1:T(2,128)S(1)}, f32[8,2]{0,1:T(2,128)}, u32[]{:S(2)}) copy-start(f32[8,2]{0,1:T(2,128)} %param.20) | copy-start | bytes 196
  1.5 1.0 %copy-start = (bf16[9,128,128]{2,1,0:T(8,128)(2,1)S(1)}, bf16[9,128,128]{2,1,0:T(8,128)(2,1)}, u32[]{:S(2)}) copy-start(bf16[9,128,128]{2,1,0:T(8,128)(2,1)} %wf_hbm.1) | copy-start | bytes 884740
  2.4 1.0 %copy-start.1 = (bf16[9,128,128]{2,1,0:T(8,128)(2,1)S(1)}, bf16[9,128,128]{2,1,0:T(8,128)(2,1)}, u32[]{:S(2)}) copy-start(bf16[9,128,128]{2,1,0:T(8,128)(2,1)} %wc_hbm.1) | copy-start | bytes 884740
  3.4 0.9 %copy-start.2 = (bf16[2,8,32,256]{3,2,1,0:T(8,128)(2,1)S(1)}, bf16[2,8,32,256]{3,2,1,0:T(8,128)(2,1)}, u32[]{:S(2)}) copy-start(bf16[2,8,32,256]{3,2,1,0:T(8,128)(2,1)} %param.15) | copy-start | bytes 786436
  4.3 0.8 %copy-start.3 = (f32[128,128]{1,0:T(8,128)S(1)}, f32[128,128]{1,0:T(8,128)}, u32[]{:S(2)}) copy-start(f32[128,128]{1,0:T(8,128)} %wt_ref.1) | copy-start | bytes 196612

commit v4 on v3

--- a/solution.py
+++ b/solution.py
@@ -18,9 +18,8 @@
 H = N // 2
 NT = 16
 NM = 8
-DUMMY = H + 1
+NY = NM // 2
 FIRST = 10
-EARLY = 4
 CHUNK = 128
 
 
@@ -41,8 +40,9 @@
 
 
 def act(x, ones, half_gain):
-    mean = dot((x * x).astype(BF16), ones)
-    h = x * lax.rsqrt(mean + 1e-06) * half_gain
+    short = x.astype(BF16)
+    mean = dot(short * short, ones)
+    h = x.astype(F32) * lax.rsqrt(mean + 1e-06) * half_gain
     return (h + h * jnp.tanh(h)).astype(BF16)
 
 
@@ -111,8 +111,8 @@
     gc_ref,
     go_ref,
     wo_ref,
-    den_ref,
-    stat_ref,
+    den_hbm,
+    stat_hbm,
     wf_ref,
     wc_ref,
     nx,
@@ -143,13 +143,17 @@
     g0,
     g1,
     act_s,
-    d_ref,
+    d_ref0,
+    d_ref1,
+    by_row,
+    den_ref,
+    stat_ref,
     send,
     recv,
-    tgt,
-    mrecv,
-    gat,
+    target,
+    other,
     w_sem,
+    o_sem,
     h_send,
     h_recv,
     c_send,
@@ -158,19 +162,22 @@
     a_recv,
     m_send,
     m_recv,
-    g_send,
-    g_recv,
+    x_send,
+    x_recv,
 ):
     pos = lax.axis_index("tile")
     mem = lax.axis_index("mem")
     started, a1, fine = (started0, started1), (a10, a11), (fine0, fine1)
     pooled, a2, coarse = (pooled0, pooled1), (a20, a21), (coarse0, coarse1)
+    d_ref = (d_ref0, d_ref1)
 
     def along_tile(d):
         return {"tile": lax.rem(pos + d, NT)}
 
-    def along_mem(d):
-        return {"mem": lax.rem(mem + d, NM)}
+    def along_y(d):
+        return {"mem": lax.rem(mem + 2 * d, NM)}
+
+    other_core = {"mem": mem + 1 - 2 * lax.rem(mem, 2)}
 
     barrier = pltpu.get_barrier_semaphore()
 
@@ -178,7 +185,8 @@
         pl.semaphore_signal(barrier, inc=1, device_id=where, device_id_type=MESH)
 
     each(NT, lambda d: greet(along_tile(d)))
-    each(NM, lambda d: greet(along_mem(d)))
+    each(NY, lambda d: greet(along_y(d)))
+    greet(other_core)
 
     load_fine = pltpu.make_async_copy(wf_hbm, wf_ref, w_sem.at[0])
     load_coarse = pltpu.make_async_copy(wc_hbm, wc_ref, w_sem.at[1])
@@ -232,22 +240,43 @@
         sx[m * 256 : (m + 1) * 256, :] = (moved * c_in[m]).astype(BF16)
 
     def lift(m):
-        def body(step, _):
-            for q in (2 * step, 2 * step + 1):
-                for half in range(2):
-                    pair = half * 8 + q
-                    cells = sx[m * 256 : (m + 1) * 256, half * 128 : (half + 1) * 128]
-                    first = (dot(cells, lift_w[q]) + temb[m]).astype(BF16)
-                    started[m][2 * pair] = first[:, :128]
-                    started[m][2 * pair + 1] = first[:, 128:]
-                    normed = act(first.astype(F32), ones_ref[...], gain_fine)
-                    a1[m][2 * pair + 1, B : B + 256, :] = normed[:, :128]
-                    a1[m][2 * pair + 2, B : B + 256, :] = normed[:, 128:]
-            return 0
-
-        lax.fori_loop(0, 4, body, 0)
+        for q in range(8):
+            for half in range(2):
+                pair = half * 8 + q
+                cells = sx[m * 256 : (m + 1) * 256, half * 128 : (half + 1) * 128]
+                first = (dot(cells, lift_w[q]) + temb[m]).astype(BF16)
+                started[m][2 * pair] = first[:, :128]
+                started[m][2 * pair + 1] = first[:, 128:]
+                normed = act(first, ones_ref[...], gain_fine)
+                a1[m][2 * pair + 1, B : B + 256, :] = normed[:, :128]
+                a1[m][2 * pair + 2, B : B + 256, :] = normed[:, 128:]
 
     lift(0)
+
+    pl.semaphore_wait(barrier, NT - 1 + NY)
+
+    def h_copy(side):
+        return pltpu.make_async_remote_copy(
+            src_ref=nx.at[:, pl.ds(side * 128, 128)],
+            dst_ref=halo.at[side],
+            send_sem=h_send.at[side],
+            recv_sem=h_recv.at[side],
+            device_id=along_tile(1 if side else NT - 1),
+            device_id_type=MESH,
+        )
+
+    def c_copy(m, side):
+        return pltpu.make_async_remote_copy(
+            src_ref=edges.at[m, side],
+            dst_ref=halo2.at[m, side],
+            send_sem=c_send.at[m, side],
+            recv_sem=c_recv.at[m, side],
+            device_id=along_tile(1 if side else NT - 1),
+            device_id_type=MESH,
+        )
+
+    for side in range(2):
+        h_copy(side).start()
 
     half = iota((B, 1), 0) >> 3
     own = iota((B, 1), 0) & 7
@@ -290,90 +319,8 @@
     load_fine.wait()
     conv_weights(fine_w, wf_ref)
     lift(1)
-
-    pl.semaphore_wait(barrier, NT - 1 + NM - 1)
-
-    def h_copy(side):
-        return pltpu.make_async_remote_copy(
-            src_ref=nx.at[:, pl.ds(side * 128, 128)],
-            dst_ref=halo.at[side],
-            send_sem=h_send.at[side],
-            recv_sem=h_recv.at[side],
-            device_id=along_tile(1 if side else NT - 1),
-            device_id_type=MESH,
-        )
-
-    def c_copy(m, side):
-        return pltpu.make_async_remote_copy(
-            src_ref=edges.at[m, side],
-            dst_ref=halo2.at[m, side],
-            send_sem=c_send.at[m, side],
-            recv_sem=c_recv.at[m, side],
-            device_id=along_tile(1 if side else NT - 1),
-            device_id_type=MESH,
-        )
-
-    for side in range(2):
-        h_copy(side).start()
-
-    def fine_post(m, pair, buf):
-        base = jnp.concatenate([started[m][2 * pair], started[m][2 * pair + 1]], axis=1)
-        out = (base.astype(F32) + buf[...]).astype(BF16)
-        fine[m][2 * pair] = out[:, :128]
-        fine[m][2 * pair + 1] = out[:, 128:]
-        wide = out.astype(F32).reshape(H // 2, 2, B, 256)
-        tall = wide[:, 0] + wide[:, 1]
-        mean = ((tall[:, :, :128] + tall[:, :, 128:]) * 0.25).reshape(128, 128).astype(BF16)
-        pooled[m][pair] = mean
-        a2[m][pair + 1, B : B + 128, :] = act(mean.astype(F32), ones_ref[0:128, 0:128], gain_coarse)
-
-    def fine_pairs(m, count, nth):
-        def body(q, _):
-            g0[...] = conv_pair(a1[m], fine_w, nth(2 * q), 256)
-            fine_post(m, jnp.where(q == 0, DUMMY, nth(2 * q - 1)), g1)
-            g1[...] = conv_pair(a1[m], fine_w, nth(2 * q + 1), 256)
-            fine_post(m, nth(2 * q), g0)
-            return 0
-
-        lax.fori_loop(0, count // 2, body, 0)
-        fine_post(m, nth(count - 1), g1)
-
-    def ends(i):
-        return i * (H - 1)
-
-    def send_edges(m):
-        edges[m, 0] = a2[m][1, B : B + 128, :]
-        edges[m, 1] = a2[m][H, B : B + 128, :]
-        for side in range(2):
-            c_copy(m, side).start()
-
-    g1[...] = jnp.zeros((256, 256), F32)
-    fine_pairs(0, H - 2, lambda i: i + 1)
-
     north_south(a11, N, H)
-    for side in range(2):
-        h_copy(side).wait()
-    sides = []
-    for side, got, w in ((3, 1, lift_w[7, :, 128:256]), (1, 0, lift_w[0, :, 0:128])):
-        both = jnp.concatenate([halo[got, 0:256, :], halo[got, 256:512, :]], axis=1)
-        moved = jnp.concatenate(from_side(seam_w.at[side], both, H, flipped[side]), axis=0)
-        sides.append(
-            [
-                dot((moved[:, m * 128 : (m + 1) * 128] * c_in[m][:, :128]).astype(BF16), w)
-                for m in range(2)
-            ]
-        )
-    for m in range(2):
-        first = (jnp.concatenate([sides[0][m], sides[1][m]], axis=1) + temb[m]).astype(BF16)
-        normed = act(first.astype(F32), ones_ref[...], gain_fine)
-        a1[m][0, B : B + 256, :] = normed[:, :128]
-        a1[m][N + 1, B : B + 256, :] = normed[:, 128:]
-        corners(a1[m], N, H)
-
-    fine_pairs(0, 2, ends)
-    send_edges(0)
-    fine_pairs(1, 2, ends)
-    send_edges(1)
+
     load_coarse.wait()
     conv_weights(coarse_w, wc_ref)
     for q in range(8):
@@ -406,10 +353,78 @@
     block = dot(block.astype(BF16), pick)[0:1, :]
     i, j = iota((64, 512), 0), iota((64, 512), 1)
     sum_ref[...] = onehot(
-        (((i & 3) + 1).astype(F32) == block)
-        & (((i >> 2) & 1) == ((j >> 3) & 1))
-        & ((i >> 3) == (j & 7))
+        (((i >> 4) + 1).astype(F32) == block)
+        & (((i >> 3) & 1) == ((j >> 3) & 1))
+        & ((i & 7) == (j & 7))
     )
+
+    def fine_post(m, pair, buf):
+        base = jnp.concatenate([started[m][2 * pair], started[m][2 * pair + 1]], axis=1)
+        out = (base.astype(F32) + buf[...]).astype(BF16)
+        fine[m][2 * pair] = out[:, :128]
+        fine[m][2 * pair + 1] = out[:, 128:]
+        wide = out.astype(F32).reshape(H // 2, 2, B, 256)
+        tall = wide[:, 0] + wide[:, 1]
+        mean = ((tall[:, :, :128] + tall[:, :, 128:]) * 0.25).reshape(128, 128).astype(BF16)
+        pooled[m][pair] = mean
+        a2[m][pair + 1, B : B + 128, :] = act(mean, ones_ref[0:128, 0:128], gain_coarse)
+
+    bufs = (g0, g1)
+    waiting = []
+
+    def finish():
+        if waiting:
+            m, pair, slot = waiting.pop()
+            fine_post(m, pair, bufs[slot])
+
+    def fine_next(m, pair):
+        slot = 1 - waiting[0][2] if waiting else 0
+        bufs[slot][...] = conv_pair(a1[m], fine_w, pair, 256)
+        finish()
+        waiting.append((m, pair, slot))
+
+    def fine_run(count):
+        m, first, slot = waiting.pop()
+
+        def body(q, _):
+            for u in range(4):
+                here, there = (slot + u) % 2, (slot + u + 1) % 2
+                pair = first + 4 * q + u
+                bufs[there][...] = conv_pair(a1[m], fine_w, pair + 1, 256)
+                fine_post(m, pair, bufs[here])
+            return 0
+
+        lax.fori_loop(0, count // 4, body, 0)
+        waiting.append((m, first + count, slot))
+
+    def send_edges(m):
+        edges[m, 0] = a2[m][1, B : B + 128, :]
+        edges[m, 1] = a2[m][H, B : B + 128, :]
+        for side in range(2):
+            c_copy(m, side).start()
+
+    fine_next(0, 1)
+    fine_run(4)
+    finish()
+
+    for side in range(2):
+        h_copy(side).wait()
+    sides = []
+    for side, got, w in ((3, 1, lift_w[7, :, 128:256]), (1, 0, lift_w[0, :, 0:128])):
+        both = jnp.concatenate([halo[got, 0:256, :], halo[got, 256:512, :]], axis=1)
+        moved = jnp.concatenate(from_side(seam_w.at[side], both, H, flipped[side]), axis=0)
+        sides.append(
+            [
+                dot((moved[:, m * 128 : (m + 1) * 128] * c_in[m][:, :128]).astype(BF16), w)
+                for m in range(2)
+            ]
+        )
+    for m in range(2):
+        first = (jnp.concatenate([sides[0][m], sides[1][m]], axis=1) + temb[m]).astype(BF16)
+        normed = act(first, ones_ref[...], gain_fine)
+        a1[m][0, B : B + 256, :] = normed[:, :128]
+        a1[m][N + 1, B : B + 256, :] = normed[:, 128:]
+        corners(a1[m], N, H)
 
     def a_copy(k, d):
         return pltpu.make_async_remote_copy(
@@ -421,23 +436,23 @@
             device_id_type=MESH,
         )
 
-    def m_copy(m, d):
+    def y_copy(m, k, d):
         return pltpu.make_async_remote_copy(
-            src_ref=tgt.at[m, lax.rem(mem + d, NM)],
-            dst_ref=mrecv.at[m, d],
-            send_sem=m_send.at[m, d],
-            recv_sem=m_recv.at[m, d],
-            device_id=along_mem(d),
+            src_ref=target.at[m, k, 0],
+            dst_ref=target.at[m, k, d],
+            send_sem=m_send.at[2 * m + k, d],
+            recv_sem=m_recv.at[2 * m + k, d],
+            device_id=along_y(d),
             device_id_type=MESH,
         )
 
-    def g_copy(d):
+    def x_copy(m, k):
         return pltpu.make_async_remote_copy(
-            src_ref=gat.at[mem],
-            dst_ref=gat.at[mem],
-            send_sem=g_send.at[d],
-            recv_sem=g_recv.at[d],
-            device_id=along_mem(d),
+            src_ref=target.at[m, k],
+            dst_ref=other.at[m, k],
+            send_sem=x_send.at[2 * m + k],
+            recv_sem=x_recv.at[2 * m + k],
+            device_id=other_core,
             device_id_type=MESH,
         )
 
@@ -481,13 +496,14 @@
         proj = jnp.concatenate([left, right], axis=1)
         cells = slice(m * 256 + start, m * 256 + start + rows)
         den = c_skip[m] * nx[cells, :].astype(F32) + c_out[m] * proj
-        d_ref[start : start + rows, :] = den
-        den_ref[cells, :] = den
+        d_ref[m][start : start + rows, :] = den
+        by_row[2 * m, start : start + rows, :] = den[:, :128]
+        by_row[2 * m + 1, start : start + rows, :] = den[:, 128:]
 
     def route_rows(m, k):
         start = k * CHUNK
-        den = d_ref[start : start + CHUNK, :].reshape(8, B, 256)
-        below = d_ref[start + B : start + B + CHUNK, :].reshape(8, B, 256)
+        den = d_ref[m][start : start + CHUNK, :].reshape(8, B, 256)
+        below = d_ref[m][start + B : start + B + CHUNK, :].reshape(8, B, 256)
         mixed = ((1.0 - frac_p) * den + frac_p * below).reshape(CHUNK, 256)
         shifted = pltpu.roll(mixed, 248, 1)
         shifted = jnp.where(iota((CHUNK, 256), 1) >= 248, mixed, shifted)
@@ -502,48 +518,87 @@
         state(m, 0, FIRST)
         route_rows(m, 0)
         state(m, FIRST, H - FIRST)
-        d_ref[H * B :, :] = jnp.concatenate([d_ref[8:16, :], d_ref[H * B - 8 : H * B, :]], axis=0)
+        d_ref[m][H * B :, :] = jnp.concatenate(
+            [d_ref[m][8:16, :], d_ref[m][H * B - 8 : H * B, :]], axis=0
+        )
         route_rows(m, 1)
 
-    def sum_stage(m):
-        for k in range(2):
-            each(NT, lambda d: a_copy(2 * m + k, d).wait_recv())
-            total = dot(sum_ref[...], recv[2 * m + k].reshape(512, 256))
-            tgt[m, :, k] = total.reshape(NM, 8, 256)
-        mrecv[m, 0] = tgt[m, mem]
-        each(NM, lambda d: m_copy(m, d).start())
-
-    fine_pairs(1, EARLY, lambda i: i + 1)
+    def sum_stage(m, k):
+        each(NT, lambda d: a_copy(2 * m + k, d).wait_recv())
+        total = dot(sum_ref[...], recv[2 * m + k].reshape(512, 256))
+        target[m, k, 0] = total.astype(BF16)
+        each(NY, lambda d: y_copy(m, k, d).start())
+
+    def pass_stage(m, k):
+        each(NY, lambda d: y_copy(m, k, d).wait_recv())
+        x_copy(m, k).start()
+
+    def stat_stage(k):
+        for m in range(2):
+            x_copy(m, k).wait_recv()
+        for q in range(4):
+            rows = slice(q * B, (q + 1) * B)
+            values = [
+                held[m, k, d, rows, :].astype(F32)
+                for held in (target, other)
+                for m in range(2)
+                for d in range(NY)
+            ]
+            mean = functools.reduce(lambda a, b: a + b, values) * (1.0 / 16)
+            squares = functools.reduce(lambda a, b: a + b, [(v - mean) * (v - mean) for v in values])
+            spread = jnp.sqrt(squares / 15.0 + 1e-06)
+            for half in range(2):
+                row = half * H + k * 8
+                stat_ref[0, q, row : row + 8, :] = mean[half * 8 : half * 8 + 8]
+                stat_ref[1, q, row : row + 8, :] = spread[half * 8 : half * 8 + 8]
+
+    fine_next(0, 0)
+    fine_next(0, H - 1)
+    fine_next(0, 6)
+    send_edges(0)
+    fine_run(8)
+    fine_next(1, 0)
+    fine_next(1, H - 1)
+    fine_next(1, 1)
+    send_edges(1)
+    fine_run(8)
+    finish()
     coarse_level(0)
     last_stage(0)
-    fine_pairs(1, H - 2 - EARLY, lambda i: i + 1 + EARLY)
+    fine_next(1, 10)
+    fine_run(4)
+    finish()
     coarse_level(1)
     last_stage(1)
-    sum_stage(0)
-    sum_stage(1)
 
     for m in range(2):
-        each(NM, lambda d: m_copy(m, d).wait_recv())
-    total = jnp.zeros((2, 8, 256), F32)
+        for b in range(B):
+            start = m * 256 + (b % 8) * N + (b // 8) * H
+            for side in range(2):
+                den_ref[start : start + H, side * 128 : (side + 1) * 128] = by_row[
+                    2 * m + side, pl.ds(b, H, stride=B), :
+                ]
+    store_den = pltpu.make_async_copy(den_ref, den_hbm, o_sem.at[0])
+    store_den.start()
+
     for m in range(2):
-        for d in range(NM):
-            total = total + mrecv[m, d]
-    mean = total * (1.0 / 16)
-    squares = jnp.zeros((2, 8, 256), F32)
+        for k in range(2):
+            sum_stage(m, k)
     for m in range(2):
-        for d in range(NM):
-            dev = mrecv[m, d] - mean
-            squares = squares + dev * dev
-    gat[mem, 0] = mean
-    gat[mem, 1] = jnp.sqrt(squares / 15.0 + 1e-06)
-    each(NM, lambda d: g_copy(d).start())
-    each(NM, lambda d: g_copy(d).wait_recv())
-    stat_ref[...] = gat[...]
+        for k in range(2):
+            pass_stage(m, k)
+    for k in range(2):
+        stat_stage(k)
+    store_stat = pltpu.make_async_copy(stat_ref, stat_hbm, o_sem.at[1])
+    store_stat.start()
     for k in range(4):
         each(NT, lambda d: a_copy(k, d).wait_send())
     for m in range(2):
-        each(NM, lambda d: m_copy(m, d).wait_send())
-    each(NM, lambda d: g_copy(d).wait_send())
+        for k in range(2):
+            each(NY, lambda d: y_copy(m, k, d).wait_send())
+            x_copy(m, k).wait_send()
+    store_den.wait()
+    store_stat.wait()
 
 
 def on_device(
@@ -571,10 +626,10 @@
         kernel,
         out_shape=(
             jax.ShapeDtypeStruct((512, 256), F32),
-            jax.ShapeDtypeStruct((NM, 2, 2, 8, 256), F32),
+            jax.ShapeDtypeStruct((2, 4, N, 256), F32),
         ),
         in_specs=[vmem, smem] + [vmem] * 6 + [hbm] * 2 + [vmem] * 4,
-        out_specs=(vmem, vmem),
+        out_specs=(hbm, hbm),
         scratch_shapes=[
             pltpu.VMEM((9, 128, 128), BF16),
             pltpu.VMEM((9, 128, 128), BF16),
@@ -590,11 +645,11 @@
             pltpu.VMEM((64, 512), BF16),
             pltpu.VMEM((2, 512, 128), BF16),
         ]
-        + [pltpu.VMEM((2 * DUMMY + 2, 256, 128), BF16)] * 2
+        + [pltpu.VMEM((N, 256, 128), BF16)] * 2
         + [pltpu.VMEM((N + 2, 288, 128), BF16)] * 2
-        + [pltpu.VMEM((2 * DUMMY + 2, 256, 128), BF16)] * 2
-        + [pltpu.VMEM((DUMMY + 1, 128, 128), BF16)] * 2
-        + [pltpu.VMEM((DUMMY + 2, 160, 128), BF16)] * 2
+        + [pltpu.VMEM((N, 256, 128), BF16)] * 2
+        + [pltpu.VMEM((H, 128, 128), BF16)] * 2
+        + [pltpu.VMEM((H + 2, 160, 128), BF16)] * 2
         + [pltpu.VMEM((H, 128, 128), BF16)] * 2
         + [
             pltpu.VMEM((2, 2, 128, 128), BF16),
@@ -603,11 +658,15 @@
             pltpu.VMEM((256, 256), F32),
             pltpu.VMEM((FIRST * B, 4096), BF16),
             pltpu.VMEM(((H + 1) * B, 256), F32),
+            pltpu.VMEM(((H + 1) * B, 256), F32),
+            pltpu.VMEM((4, 256, 128), F32),
+            pltpu.VMEM((512, 256), F32),
+            pltpu.VMEM((2, 4, N, 256), F32),
             pltpu.VMEM((4, NT, 32, 256), BF16),
             pltpu.VMEM((4, NT, 32, 256), BF16),
-            pltpu.VMEM((2, NM, 2, 8, 256), F32),
-            pltpu.VMEM((2, NM, 2, 8, 256), F32),
-            pltpu.VMEM((NM, 2, 2, 8, 256), F32),
+            pltpu.VMEM((2, 2, NY, 64, 256), BF16),
+            pltpu.VMEM((2, 2, NY, 64, 256), BF16),
+            dma((2,)),
             dma((2,)),
             dma((2,)),
             dma((2,)),
@@ -615,13 +674,13 @@
             dma((2, 2)),
             dma((4, NT)),
             dma((4, NT)),
-            dma((2, NM)),
-            dma((2, NM)),
-            dma((NM,)),
-            dma((NM,)),
+            dma((4, NY)),
+            dma((4, NY)),
+            dma((4,)),
+            dma((4,)),
         ],
         compiler_params=pltpu.CompilerParams(
-            collective_id=0, has_side_effects=True, vmem_limit_bytes=36 * 1024 * 1024
+            collective_id=0, has_side_effects=True, vmem_limit_bytes=56 * 1024 * 1024
         ),
     )(
         noisy.reshape(512, 256),
@@ -639,9 +698,7 @@
         gain_out.reshape(1, 128),
         w_out.T,
     )
-    denoised = den.reshape(2, H, 2, 8, 256).transpose(0, 3, 2, 1, 4).reshape(noisy.shape)
-    stat = stat.reshape(NM, 2, 2, 2, 4, 256).transpose(1, 4, 3, 2, 0, 5).reshape(2, 4, N, 256)
-    return (denoised, stat[0], stat[1])
+    return (den.reshape(noisy.shape), stat[0], stat[1])
 
 
 def solution(mesh):

time: 62.7 us -> 52.3 us (0.83)
  Pallas kernels: 54.5 us -> 48.9 us
  local copies, waits for them, and re-layouts: 7.11 us -> 2.54 us
    pallas_call x1, Pallas kernels: 54.5 us -> 48.9 us  [on_device(): pl.pallas_call(kernel, out_shape=(jax.ShapeDtypeStruct((512, 256), F32),...]
    unnamed x28 -> x3, local copies, waits for them, and re-layouts: 4.45 us -> 0.8 us
    squeeze x0 -> x1, local copies, waits for them, and re-layouts: none -> 1.74 us  [on_device(): return (den.reshape(noisy.shape), stat[0], stat[1])]
    slice x3 -> x0, local copies, waits for them, and re-layouts: 1.49 us -> none  [on_device(): return (denoised, stat[0], stat[1])]
    transpose x1 -> x0, local copies, waits for them, and re-layouts: 1.1 us -> none  [on_device(): den.reshape(2, H, 2, 8, 256).transpose(0, 3, 2, 1, 4).reshape(noisy.shape)]
where the time goes in v4:
time: 52.3 us; the launch traced here: 52.1 us
  Pallas kernels  48.9 us (93%)
  local copies, waits for them, and re-layouts  2.54 us (5%)
  between operations  0.65 us (1%)
    pallas_call x1, Pallas kernels, on_device(): pl.pallas_call(kernel, out_shape=(jax.ShapeDtypeStruct((512, 256), F32),...  48.9 us
    squeeze x1, local copies, waits for them, and re-layouts, on_device(): return (den.reshape(noisy.shape), stat[0], stat[1])  1.74 us

profile of v4, /device:TPU:1, one launch (start us, length us, event | category | flops | bytes accessed | tf_op | source)
XLA Modules:
  0.0 52.1 jit_solution(3846434912452925380)
XLA Ops:
  0.6 48.9 %shard_map.157 = (f32[512,256]{1,0:T(8,128)}, f32[2,4,32,256]{3,2,1,0:T(8,128)}) custom-call(bf16[512,256]{1,0:T(8,128)(2,1)} %bitcast.15, s32[2]{0:T(128)} %step_ref.1, s32[3,4,8]{2,1,0:T(4,128)} %bitcast.16, s32[1,128]{1,0:T(1,128)} %bitcast.19, s32[1,128]{1,0:T(1,128)} %bitcast.20, f32[2,8]{1,0:T(2,128)} %bitcast.18, f32[128,128]{1,0:T(8,128)} %wt_ref.1, ...), custom_call_target="tpu_custom_call" | custom-call | tf_op jit(solution)/shard_map/pallas_call | solution.py:625
  49.6 0.0 copy-start
  49.6 1.7 %slice_bitcast_fusion = (f32[4,32,256]{2,1,0:T(8,128)}, f32[4,32,256]{2,1,0:T(8,128)}) fusion(f32[2,4,32,256]{3,2,1,0:T(8,128)} %get-tuple-element.6), kind=kLoop, calls=%fused_computation | loop fusion | bytes 524288 | tf_op jit(solution)/shard_map/squeeze | solution.py:701
  51.3 0.0 copy-done
  51.3 0.8 %copy.18 = f32[2,8,32,256]{3,2,1,0:T(8,128)} copy(f32[2,8,32,256]{3,2,1,0:T(8,128)S(1)} %bitcast.14) | data formatting | bytes 1048576
Async XLA Ops:
  49.6 1.8 %copy-start = (f32[512,256]{1,0:T(8,128)S(1)}, f32[512,256]{1,0:T(8,128)}, u32[]{:S(2)}) copy-start(f32[512,256]{1,0:T(8,128)} %get-tuple-element.5) | copy-start | bytes 1572868

commit v5 on v4

--- a/solution.py
+++ b/solution.py
@@ -19,7 +19,9 @@
 NT = 16
 NM = 8
 NY = NM // 2
+FAR = sorted(range(1, NT), key=lambda e: -min(e // 4, 4 - e // 4) - min(e % 4, 4 - e % 4))
 FIRST = 10
+EARLY = 5
 CHUNK = 128
 
 
@@ -97,6 +99,23 @@
 
 
 def kernel(
+    noisy_hbm,
+    step_hbm,
+    seam_hbm,
+    route_hbm,
+    block_hbm,
+    frac_hbm,
+    wt_hbm,
+    wl_hbm,
+    wf_hbm,
+    wc_hbm,
+    gf_hbm,
+    gc_hbm,
+    go_hbm,
+    wo_hbm,
+    den_hbm,
+    mean_hbm,
+    spread_hbm,
     noisy_ref,
     step_ref,
     seam_ref,
@@ -105,16 +124,12 @@
     frac_ref,
     wt_ref,
     wl_ref,
-    wf_hbm,
-    wc_hbm,
+    wf_ref,
+    wc_ref,
     gf_ref,
     gc_ref,
     go_ref,
     wo_ref,
-    den_hbm,
-    stat_hbm,
-    wf_ref,
-    wc_ref,
     nx,
     sx,
     lift_w,
@@ -147,7 +162,8 @@
     d_ref1,
     by_row,
     den_ref,
-    stat_ref,
+    mean_ref,
+    spread_ref,
     send,
     recv,
     target,
@@ -174,6 +190,9 @@
     def along_tile(d):
         return {"tile": lax.rem(pos + d, NT)}
 
+    def torus(e):
+        return {"tile": lax.rem(pos // 4 + e // 4, 4) * 4 + lax.rem(lax.rem(pos, 4) + e % 4, 4)}
+
     def along_y(d):
         return {"mem": lax.rem(mem + 2 * d, NM)}
 
@@ -188,14 +207,31 @@
     each(NY, lambda d: greet(along_y(d)))
     greet(other_core)
 
-    load_fine = pltpu.make_async_copy(wf_hbm, wf_ref, w_sem.at[0])
-    load_coarse = pltpu.make_async_copy(wc_hbm, wc_ref, w_sem.at[1])
-    load_fine.start()
-    load_coarse.start()
+    inputs = (
+        (noisy_hbm, noisy_ref),
+        (step_hbm, step_ref),
+        (wt_hbm, wt_ref),
+        (wl_hbm, wl_ref),
+        (gf_hbm, gf_ref),
+        (seam_hbm, seam_ref),
+        (wf_hbm, wf_ref),
+        (gc_hbm, gc_ref),
+        (go_hbm, go_ref),
+        (route_hbm, route_ref),
+        (block_hbm, block_ref),
+        (frac_hbm, frac_ref),
+        (wo_hbm, wo_ref),
+        (wc_hbm, wc_ref),
+    )
+    loads = [pltpu.make_async_copy(a, b, w_sem.at[i]) for i, (a, b) in enumerate(inputs)]
+    for load in loads:
+        load.start()
 
     ones_ref[...] = jnp.where(
         iota((256, 256), 0) // 128 == iota((256, 256), 1) // 128, 1.0 / 128, 0.0
     ).astype(BF16)
+    for load in loads[:6]:
+        load.wait()
     wl = wl_ref[...].astype(F32)
     wl_zero = jnp.zeros_like(wl)
     wl_pair = jnp.concatenate(
@@ -209,7 +245,7 @@
         lift_w[q] = jnp.zeros((128, 256), BF16)
         lift_w[q, q * B : (q + 1) * B, :] = wl_pair
 
-    level = jnp.where(iota((8, 128), 0) < 4, step_ref[0], step_ref[1]).astype(F32)
+    level = jnp.where(iota((8, 128), 0) < 4, step_ref[0:1, 0:1], step_ref[0:1, 1:2]).astype(F32)
     fraction = level / (STEPS - 1)
     high_root = 80.0 ** (1.0 / 7.0)
     low_root = 0.002 ** (1.0 / 7.0)
@@ -229,8 +265,6 @@
     embedded = embedded / (1.0 + jnp.exp(-embedded))
     temb = [twice(embedded[0:1]), twice(embedded[4:5])]
     gain_fine = twice(gf_ref[...]) * 0.5
-    gain_coarse = gc_ref[...] * 0.5
-    gain_out = twice(go_ref[...]) * 0.5
 
     i = iota((256, 256), 0)
     to_rows = onehot(((i & 7) * N + ((i >> 3) & 1) * H + (i >> 4)) == iota((256, 256), 1))
@@ -316,12 +350,13 @@
             ).astype(BF16)
 
     north_south(a10, N, H)
-    load_fine.wait()
+    loads[6].wait()
     conv_weights(fine_w, wf_ref)
-    lift(1)
-    north_south(a11, N, H)
-
-    load_coarse.wait()
+
+    for load in loads[7:]:
+        load.wait()
+    gain_coarse = gc_ref[...] * 0.5
+    gain_out = twice(go_ref[...]) * 0.5
     conv_weights(coarse_w, wc_ref)
     for q in range(8):
         for j in range(2):
@@ -338,14 +373,17 @@
     for s in range(1, 8):
         again = (pltpu.roll(route, s, 1) == route) & ((lane & 7) >= s)
         rank = rank + jnp.where(again, 1, 0)
-    key = ((route - pos) & (NT - 1)) * 2 + rank
+    def offset(to, start):
+        return (((to >> 2) - (start >> 2)) & 3) * 4 + ((to - start) & 3)
+
+    key = offset(route, pos) * 2 + rank
     pick = onehot(iota((128, 128), 0) == pos * 8 + (iota((128, 128), 1) & 7))
     key = dot(key.astype(F32).astype(BF16), pick)[0:1, :]
     i, j = iota((512, 128), 0), iota((512, 128), 1)
     slot_ref[...] = onehot(
         ((i >> 4).astype(F32) == key) & (((i >> 3) & 1) == ((j >> 3) & 1)) & ((i & 7) == (j >> 4))
     )
-    slot = jnp.where(route == pos, ((pos - (lane >> 3)) & (NT - 1)) * 2 + rank, -1).astype(F32)
+    slot = jnp.where(route == pos, offset(pos, lane >> 3) * 2 + rank, -1).astype(F32)
     diagonal = iota((128, 128), 0) == iota((128, 128), 1)
     slot = jnp.sum(jnp.where(diagonal, slot[0:1, :], 0.0), axis=1, keepdims=True)
     pick = onehot(slot == (iota((128, 512), 1) >> 4).astype(F32))
@@ -384,18 +422,9 @@
         waiting.append((m, pair, slot))
 
     def fine_run(count):
-        m, first, slot = waiting.pop()
-
-        def body(q, _):
-            for u in range(4):
-                here, there = (slot + u) % 2, (slot + u + 1) % 2
-                pair = first + 4 * q + u
-                bufs[there][...] = conv_pair(a1[m], fine_w, pair + 1, 256)
-                fine_post(m, pair, bufs[here])
-            return 0
-
-        lax.fori_loop(0, count // 4, body, 0)
-        waiting.append((m, first + count, slot))
+        for _ in range(count):
+            m, pair, _ = waiting[0]
+            fine_next(m, pair + 1)
 
     def send_edges(m):
         edges[m, 0] = a2[m][1, B : B + 128, :]
@@ -404,7 +433,7 @@
             c_copy(m, side).start()
 
     fine_next(0, 1)
-    fine_run(4)
+    fine_run(H - 3)
     finish()
 
     for side in range(2):
@@ -419,7 +448,7 @@
                 for m in range(2)
             ]
         )
-    for m in range(2):
+    def east_west(m):
         first = (jnp.concatenate([sides[0][m], sides[1][m]], axis=1) + temb[m]).astype(BF16)
         normed = act(first, ones_ref[...], gain_fine)
         a1[m][0, B : B + 256, :] = normed[:, :128]
@@ -432,7 +461,7 @@
             dst_ref=recv.at[k, d],
             send_sem=a_send.at[k, d],
             recv_sem=a_recv.at[k, d],
-            device_id=along_tile(d),
+            device_id=torus(d),
             device_id_type=MESH,
         )
 
@@ -512,7 +541,8 @@
         blocks = blocks.reshape(NT, 32, 256)
         recv[2 * m + k, 0] = blocks[0]
         send[2 * m + k] = blocks
-        each(NT, lambda d: a_copy(2 * m + k, d).start())
+        for d in FAR:
+            a_copy(2 * m + k, d).start()
 
     def last_stage(m):
         state(m, 0, FIRST)
@@ -549,24 +579,27 @@
             spread = jnp.sqrt(squares / 15.0 + 1e-06)
             for half in range(2):
                 row = half * H + k * 8
-                stat_ref[0, q, row : row + 8, :] = mean[half * 8 : half * 8 + 8]
-                stat_ref[1, q, row : row + 8, :] = spread[half * 8 : half * 8 + 8]
-
+                mean_ref[q, row : row + 8, :] = mean[half * 8 : half * 8 + 8]
+                spread_ref[q, row : row + 8, :] = spread[half * 8 : half * 8 + 8]
+
+    east_west(0)
     fine_next(0, 0)
     fine_next(0, H - 1)
-    fine_next(0, 6)
+    finish()
     send_edges(0)
-    fine_run(8)
+    lift(1)
+    north_south(a11, N, H)
+    east_west(1)
     fine_next(1, 0)
     fine_next(1, H - 1)
     fine_next(1, 1)
     send_edges(1)
-    fine_run(8)
+    fine_run(EARLY - 1)
     finish()
     coarse_level(0)
     last_stage(0)
-    fine_next(1, 10)
-    fine_run(4)
+    fine_next(1, EARLY + 1)
+    fine_run(H - 3 - EARLY)
     finish()
     coarse_level(1)
     last_stage(1)
@@ -589,8 +622,10 @@
             pass_stage(m, k)
     for k in range(2):
         stat_stage(k)
-    store_stat = pltpu.make_async_copy(stat_ref, stat_hbm, o_sem.at[1])
-    store_stat.start()
+    store_mean = pltpu.make_async_copy(mean_ref, mean_hbm, o_sem.at[1])
+    store_spread = pltpu.make_async_copy(spread_ref, spread_hbm, o_sem.at[2])
+    store_mean.start()
+    store_spread.start()
     for k in range(4):
         each(NT, lambda d: a_copy(k, d).wait_send())
     for m in range(2):
@@ -598,7 +633,8 @@
             each(NY, lambda d: y_copy(m, k, d).wait_send())
             x_copy(m, k).wait_send()
     store_den.wait()
-    store_stat.wait()
+    store_mean.wait()
+    store_spread.wait()
 
 
 def on_device(
@@ -618,21 +654,32 @@
     gain_out,
     w_out,
 ):
-    vmem = pl.BlockSpec(memory_space=pltpu.VMEM)
-    smem = pl.BlockSpec(memory_space=pltpu.SMEM)
     hbm = pl.BlockSpec(memory_space=pltpu.HBM)
     dma = pltpu.SemaphoreType.DMA
-    den, stat = pl.pallas_call(
+    den, mean, spread = pl.pallas_call(
         kernel,
         out_shape=(
             jax.ShapeDtypeStruct((512, 256), F32),
-            jax.ShapeDtypeStruct((2, 4, N, 256), F32),
+            jax.ShapeDtypeStruct((4, N, 256), F32),
+            jax.ShapeDtypeStruct((4, N, 256), F32),
         ),
-        in_specs=[vmem, smem] + [vmem] * 6 + [hbm] * 2 + [vmem] * 4,
-        out_specs=(hbm, hbm),
+        in_specs=[hbm] * 14,
+        out_specs=(hbm, hbm, hbm),
         scratch_shapes=[
+            pltpu.VMEM((512, 256), BF16),
+            pltpu.VMEM((1, 2), jnp.int32),
+            pltpu.VMEM((3, 4, 8), jnp.int32),
+            pltpu.VMEM((1, 128), jnp.int32),
+            pltpu.VMEM((1, 128), jnp.int32),
+            pltpu.VMEM((2, 8), F32),
+            pltpu.VMEM((128, 128), F32),
+            pltpu.VMEM((8, 128), BF16),
             pltpu.VMEM((9, 128, 128), BF16),
             pltpu.VMEM((9, 128, 128), BF16),
+            pltpu.VMEM((1, 128), F32),
+            pltpu.VMEM((1, 128), F32),
+            pltpu.VMEM((1, 128), F32),
+            pltpu.VMEM((8, 128), BF16),
             pltpu.VMEM((512, 256), BF16),
             pltpu.VMEM((512, 256), BF16),
             pltpu.VMEM((8, 128, 256), BF16),
@@ -661,13 +708,14 @@
             pltpu.VMEM(((H + 1) * B, 256), F32),
             pltpu.VMEM((4, 256, 128), F32),
             pltpu.VMEM((512, 256), F32),
-            pltpu.VMEM((2, 4, N, 256), F32),
+            pltpu.VMEM((4, N, 256), F32),
+            pltpu.VMEM((4, N, 256), F32),
             pltpu.VMEM((4, NT, 32, 256), BF16),
             pltpu.VMEM((4, NT, 32, 256), BF16),
             pltpu.VMEM((2, 2, NY, 64, 256), BF16),
             pltpu.VMEM((2, 2, NY, 64, 256), BF16),
-            dma((2,)),
-            dma((2,)),
+            dma((14,)),
+            dma((3,)),
             dma((2,)),
             dma((2,)),
             dma((2, 2)),
@@ -684,7 +732,7 @@
         ),
     )(
         noisy.reshape(512, 256),
-        timestep,
+        timestep.reshape(1, 2),
         seams.transpose(2, 1, 0),
         route.reshape(1, 128),
         target_block.reshape(1, 128),
@@ -698,7 +746,7 @@
         gain_out.reshape(1, 128),
         w_out.T,
     )
-    return (den.reshape(noisy.shape), stat[0], stat[1])
+    return (den.reshape(noisy.shape), mean, spread)
 
 
 def solution(mesh):

time: 52.3 us -> 52 us (level)
  Pallas kernels: 48.9 us -> 47.6 us
  local copies, waits for them, and re-layouts: 2.54 us -> 3.53 us
    unnamed x3 -> x7, local copies, waits for them, and re-layouts: 0.8 us -> 3.53 us
    squeeze x1 -> x0, local copies, waits for them, and re-layouts: 1.74 us -> none  [on_device(): return (den.reshape(noisy.shape), stat[0], stat[1])]
    pallas_call x1, Pallas kernels: 48.9 us -> 47.6 us  [on_device(): pl.pallas_call(kernel, out_shape=(jax.ShapeDtypeStruct((512, 256), F32),...]
where the time goes in v5:
time: 52 us; the launch traced here: 51.8 us
  Pallas kernels  47.6 us (92%)
  local copies, waits for them, and re-layouts  3.53 us (7%)
  between operations  0.66 us (1%)
    pallas_call x1, Pallas kernels, on_device(): pl.pallas_call(kernel, out_shape=(jax.ShapeDtypeStruct((512, 256), F32),...  47.6 us
    unnamed x7, local copies, waits for them, and re-layouts  3.53 us

profile of v5, /device:TPU:1, one launch (start us, length us, event | category | flops | bytes accessed | tf_op | source)
XLA Modules:
  0.0 51.8 jit_solution(13263229534240945448)
XLA Ops:
  0.6 47.6 %shard_map.157 = (f32[512,256]{1,0:T(8,128)}, f32[4,32,256]{2,1,0:T(8,128)}, f32[4,32,256]{2,1,0:T(8,128)}) custom-call(bf16[512,256]{1,0:T(8,128)(2,1)} %bitcast.12, s32[1,2]{1,0:T(1,128)} %bitcast.16, s32[3,4,8]{2,1,0:T(4,128)} %bitcast.13, s32[1,128]{1,0:T(1,128)} %bitcast.17, s32[1,128]{1,0:T(1,128)} %bitcast.18, f32[2,8]{1,0:T(2,128)} %bitcast.15, ...), custom_call_target="tpu_custom_call" | custom-call | tf_op jit(solution)/shard_map/pallas_call | solution.py:659
  48.3 0.0 copy-start.1
  48.3 1.9 %copy.20 = f32[2,8,32,256]{3,2,1,0:T(8,128)} copy(f32[2,8,32,256]{3,2,1,0:T(8,128)} %bitcast.11) | data formatting | bytes 1048576
  50.2 0.0 copy-done.1
  50.2 0.0 copy-start
  50.2 0.7 %copy.21 = f32[4,32,256]{2,1,0:T(8,128)} copy(f32[4,32,256]{2,1,0:T(8,128)S(1)} %copy-done.1) | data formatting | bytes 262144
  50.9 0.3 copy-done
  51.2 0.7 %copy.22 = f32[4,32,256]{2,1,0:T(8,128)} copy(f32[4,32,256]{2,1,0:T(8,128)S(1)} %copy-done) | data formatting | bytes 262144
Async XLA Ops:
  48.3 1.9 %copy-start.1 = (f32[4,32,256]{2,1,0:T(8,128)S(1)}, f32[4,32,256]{2,1,0:T(8,128)}, u32[]{:S(2)}) copy-start(f32[4,32,256]{2,1,0:T(8,128)} %get-tuple-element.13) | copy-start | bytes 393220
  50.2 1.0 %copy-start = (f32[4,32,256]{2,1,0:T(8,128)S(1)}, f32[4,32,256]{2,1,0:T(8,128)}, u32[]{:S(2)}) copy-start(f32[4,32,256]{2,1,0:T(8,128)} %get-tuple-element.14) | copy-start | bytes 393220

commit v6 on v5

--- a/solution.py
+++ b/solution.py
@@ -21,7 +21,7 @@
 NY = NM // 2
 FAR = sorted(range(1, NT), key=lambda e: -min(e // 4, 4 - e // 4) - min(e % 4, 4 - e % 4))
 FIRST = 10
-EARLY = 5
+EARLY = 9
 CHUNK = 128
 
 
@@ -114,8 +114,7 @@
     go_hbm,
     wo_hbm,
     den_hbm,
-    mean_hbm,
-    spread_hbm,
+    stat_hbm,
     noisy_ref,
     step_ref,
     seam_ref,
@@ -196,6 +195,10 @@
     def along_y(d):
         return {"mem": lax.rem(mem + 2 * d, NM)}
 
+    def across(d):
+        there = lax.rem(mem + 2 * d, NM)
+        return {"mem": there + 1 - 2 * lax.rem(there, 2)}
+
     other_core = {"mem": mem + 1 - 2 * lax.rem(mem, 2)}
 
     barrier = pltpu.get_barrier_semaphore()
@@ -205,6 +208,7 @@
 
     each(NT, lambda d: greet(along_tile(d)))
     each(NY, lambda d: greet(along_y(d)))
+    each(NY, lambda d: greet(across(d)))
     greet(other_core)
 
     inputs = (
@@ -230,6 +234,9 @@
     ones_ref[...] = jnp.where(
         iota((256, 256), 0) // 128 == iota((256, 256), 1) // 128, 1.0 / 128, 0.0
     ).astype(BF16)
+    i = iota((256, 256), 0)
+    to_rows = onehot(((i & 7) * N + ((i >> 3) & 1) * H + (i >> 4)) == iota((256, 256), 1))
+    lift_w[...] = jnp.zeros((8, 128, 256), BF16)
     for load in loads[:6]:
         load.wait()
     wl = wl_ref[...].astype(F32)
@@ -242,7 +249,6 @@
         axis=0,
     ).astype(BF16)
     for q in range(8):
-        lift_w[q] = jnp.zeros((128, 256), BF16)
         lift_w[q, q * B : (q + 1) * B, :] = wl_pair
 
     level = jnp.where(iota((8, 128), 0) < 4, step_ref[0:1, 0:1], step_ref[0:1, 1:2]).astype(F32)
@@ -266,8 +272,6 @@
     temb = [twice(embedded[0:1]), twice(embedded[4:5])]
     gain_fine = twice(gf_ref[...]) * 0.5
 
-    i = iota((256, 256), 0)
-    to_rows = onehot(((i & 7) * N + ((i >> 3) & 1) * H + (i >> 4)) == iota((256, 256), 1))
     for m in range(2):
         moved = dot(to_rows, noisy_ref[m * 256 : (m + 1) * 256, :])
         nx[m * 256 : (m + 1) * 256, :] = moved.astype(BF16)
@@ -287,7 +291,7 @@
 
     lift(0)
 
-    pl.semaphore_wait(barrier, NT - 1 + NY)
+    pl.semaphore_wait(barrier, NT - 1 + NM - 1)
 
     def h_copy(side):
         return pltpu.make_async_remote_copy(
@@ -475,13 +479,14 @@
             device_id_type=MESH,
         )
 
-    def x_copy(m, k):
+    def x_copy(m, k, d):
+        last = m == 1 and k == 1 and d > 0
         return pltpu.make_async_remote_copy(
-            src_ref=target.at[m, k],
-            dst_ref=other.at[m, k],
-            send_sem=x_send.at[2 * m + k],
-            recv_sem=x_recv.at[2 * m + k],
-            device_id=other_core,
+            src_ref=target.at[m, k, 0 if last else d],
+            dst_ref=other.at[m, k, d],
+            send_sem=x_send.at[2 * m + k, d],
+            recv_sem=x_recv.at[2 * m + k, d],
+            device_id=across(d) if last else other_core,
             device_id_type=MESH,
         )
 
@@ -557,15 +562,22 @@
         each(NT, lambda d: a_copy(2 * m + k, d).wait_recv())
         total = dot(sum_ref[...], recv[2 * m + k].reshape(512, 256))
         target[m, k, 0] = total.astype(BF16)
-        each(NY, lambda d: y_copy(m, k, d).start())
+        for d in (2, 1, 3):
+            y_copy(m, k, d).start()
+            if m == 1 and k == 1:
+                x_copy(m, k, d).start()
+        x_copy(m, k, 0).start()
 
     def pass_stage(m, k):
-        each(NY, lambda d: y_copy(m, k, d).wait_recv())
-        x_copy(m, k).start()
+        for d in (1, 3, 2):
+            y_copy(m, k, d).wait_recv()
+            if not (m == 1 and k == 1):
+                x_copy(m, k, d).start()
 
     def stat_stage(k):
         for m in range(2):
-            x_copy(m, k).wait_recv()
+            for d in range(NY):
+                x_copy(m, k, d).wait_recv()
         for q in range(4):
             rows = slice(q * B, (q + 1) * B)
             values = [
@@ -622,8 +634,8 @@
             pass_stage(m, k)
     for k in range(2):
         stat_stage(k)
-    store_mean = pltpu.make_async_copy(mean_ref, mean_hbm, o_sem.at[1])
-    store_spread = pltpu.make_async_copy(spread_ref, spread_hbm, o_sem.at[2])
+    store_mean = pltpu.make_async_copy(mean_ref, stat_hbm.at[0], o_sem.at[1])
+    store_spread = pltpu.make_async_copy(spread_ref, stat_hbm.at[1], o_sem.at[2])
     store_mean.start()
     store_spread.start()
     for k in range(4):
@@ -631,7 +643,8 @@
     for m in range(2):
         for k in range(2):
             each(NY, lambda d: y_copy(m, k, d).wait_send())
-            x_copy(m, k).wait_send()
+            for d in range(NY):
+                x_copy(m, k, d).wait_send()
     store_den.wait()
     store_mean.wait()
     store_spread.wait()
@@ -656,15 +669,14 @@
 ):
     hbm = pl.BlockSpec(memory_space=pltpu.HBM)
     dma = pltpu.SemaphoreType.DMA
-    den, mean, spread = pl.pallas_call(
+    den, stat = pl.pallas_call(
         kernel,
         out_shape=(
             jax.ShapeDtypeStruct((512, 256), F32),
-            jax.ShapeDtypeStruct((4, N, 256), F32),
-            jax.ShapeDtypeStruct((4, N, 256), F32),
+            jax.ShapeDtypeStruct((2, 4, N, 256), F32),
         ),
         in_specs=[hbm] * 14,
-        out_specs=(hbm, hbm, hbm),
+        out_specs=(hbm, hbm),
         scratch_shapes=[
             pltpu.VMEM((512, 256), BF16),
             pltpu.VMEM((1, 2), jnp.int32),
@@ -724,8 +736,8 @@
             dma((4, NT)),
             dma((4, NY)),
             dma((4, NY)),
-            dma((4,)),
-            dma((4,)),
+            dma((4, NY)),
+            dma((4, NY)),
         ],
         compiler_params=pltpu.CompilerParams(
             collective_id=0, has_side_effects=True, vmem_limit_bytes=56 * 1024 * 1024
@@ -746,7 +758,7 @@
         gain_out.reshape(1, 128),
         w_out.T,
     )
-    return (den.reshape(noisy.shape), mean, spread)
+    return (den.reshape(noisy.shape), stat[0], stat[1])
 
 
 def solution(mesh):

time: 52 us -> 50.6 us (0.973)
  local copies, waits for them, and re-layouts: 3.53 us -> 2.54 us
    unnamed x7 -> x3, local copies, waits for them, and re-layouts: 3.53 us -> 0.8 us
    squeeze x0 -> x1, local copies, waits for them, and re-layouts: none -> 1.74 us  [on_device(): return (den.reshape(noisy.shape), stat[0], stat[1])]
where the time goes in v6:
time: 50.6 us; the launch traced here: 50.4 us
  Pallas kernels  47.2 us (93%)
  local copies, waits for them, and re-layouts  2.54 us (5%)
  between operations  0.65 us (1%)
    pallas_call x1, Pallas kernels, on_device(): pl.pallas_call(kernel, out_shape=(jax.ShapeDtypeStruct((512, 256), F32),...  47.2 us
    squeeze x1, local copies, waits for them, and re-layouts, on_device(): return (den.reshape(noisy.shape), stat[0], stat[1])  1.74 us

profile of v6, /device:TPU:1, one launch (start us, length us, event | category | flops | bytes accessed | tf_op | source)
XLA Modules:
  0.0 50.4 jit_solution(184802999788455981)
XLA Ops:
  0.6 47.2 %shard_map.157 = (f32[512,256]{1,0:T(8,128)}, f32[2,4,32,256]{3,2,1,0:T(8,128)}) custom-call(bf16[512,256]{1,0:T(8,128)(2,1)} %bitcast.16, s32[1,2]{1,0:T(1,128)} %bitcast.20, s32[3,4,8]{2,1,0:T(4,128)} %bitcast.17, s32[1,128]{1,0:T(1,128)} %bitcast.21, s32[1,128]{1,0:T(1,128)} %bitcast.22, f32[2,8]{1,0:T(2,128)} %bitcast.19, f32[128,128]{1,0:T(8,128)} %wt_hbm.1, ...), custom_call_target="tpu_custom_call" | custom-call | tf_op jit(solution)/shard_map/pallas_call | solution.py:672
  47.9 0.0 copy-start
  47.9 1.7 %slice_bitcast_fusion = (f32[4,32,256]{2,1,0:T(8,128)}, f32[4,32,256]{2,1,0:T(8,128)}) fusion(f32[2,4,32,256]{3,2,1,0:T(8,128)} %get-tuple-element.6), kind=kLoop, calls=%fused_computation | loop fusion | bytes 524288 | tf_op jit(solution)/shard_map/squeeze | solution.py:761
  49.6 0.0 copy-done
  49.6 0.8 %copy.18 = f32[2,8,32,256]{3,2,1,0:T(8,128)} copy(f32[2,8,32,256]{3,2,1,0:T(8,128)S(1)} %bitcast.15) | data formatting | bytes 1048576
Async XLA Ops:
  47.9 1.8 %copy-start = (f32[512,256]{1,0:T(8,128)S(1)}, f32[512,256]{1,0:T(8,128)}, u32[]{:S(2)}) copy-start(f32[512,256]{1,0:T(8,128)} %get-tuple-element.5) | copy-start | bytes 1572868

commit v7 on v6

--- a/solution.py
+++ b/solution.py
@@ -629,11 +629,12 @@
     for m in range(2):
         for k in range(2):
             sum_stage(m, k)
-    for m in range(2):
-        for k in range(2):
-            pass_stage(m, k)
-    for k in range(2):
-        stat_stage(k)
+    pass_stage(0, 0)
+    pass_stage(0, 1)
+    pass_stage(1, 0)
+    stat_stage(0)
+    pass_stage(1, 1)
+    stat_stage(1)
     store_mean = pltpu.make_async_copy(mean_ref, stat_hbm.at[0], o_sem.at[1])
     store_spread = pltpu.make_async_copy(spread_ref, stat_hbm.at[1], o_sem.at[2])
     store_mean.start()

time: 50.6 us -> 50.6 us (level)
  no operation moved by 1% of the time
where the time goes in v7:
time: 50.6 us; the launch traced here: 50.4 us
  Pallas kernels  47.3 us (93%)
  local copies, waits for them, and re-layouts  2.54 us (5%)
  between operations  0.65 us (1%)
    pallas_call x1, Pallas kernels, on_device(): pl.pallas_call(kernel, out_shape=(jax.ShapeDtypeStruct((512, 256), F32),...  47.3 us
    squeeze x1, local copies, waits for them, and re-layouts, on_device(): return (den.reshape(noisy.shape), stat[0], stat[1])  1.74 us

profile of v7, /device:TPU:1, one launch (start us, length us, event | category | flops | bytes accessed | tf_op | source)
XLA Modules:
  0.0 50.4 jit_solution(15776507681038579166)
XLA Ops:
  0.6 47.3 %shard_map.157 = (f32[512,256]{1,0:T(8,128)}, f32[2,4,32,256]{3,2,1,0:T(8,128)}) custom-call(bf16[512,256]{1,0:T(8,128)(2,1)} %bitcast.16, s32[1,2]{1,0:T(1,128)} %bitcast.20, s32[3,4,8]{2,1,0:T(4,128)} %bitcast.17, s32[1,128]{1,0:T(1,128)} %bitcast.21, s32[1,128]{1,0:T(1,128)} %bitcast.22, f32[2,8]{1,0:T(2,128)} %bitcast.19, f32[128,128]{1,0:T(8,128)} %wt_hbm.1, ...), custom_call_target="tpu_custom_call" | custom-call | tf_op jit(solution)/shard_map/pallas_call | solution.py:673
  47.9 0.0 copy-start
  47.9 1.7 %slice_bitcast_fusion = (f32[4,32,256]{2,1,0:T(8,128)}, f32[4,32,256]{2,1,0:T(8,128)}) fusion(f32[2,4,32,256]{3,2,1,0:T(8,128)} %get-tuple-element.6), kind=kLoop, calls=%fused_computation | loop fusion | bytes 524288 | tf_op jit(solution)/shard_map/squeeze | solution.py:762
  49.6 0.0 copy-done
  49.7 0.8 %copy.18 = f32[2,8,32,256]{3,2,1,0:T(8,128)} copy(f32[2,8,32,256]{3,2,1,0:T(8,128)S(1)} %bitcast.15) | data formatting | bytes 1048576
Async XLA Ops:
  47.9 1.8 %copy-start = (f32[512,256]{1,0:T(8,128)S(1)}, f32[512,256]{1,0:T(8,128)}, u32[]{:S(2)}) copy-start(f32[512,256]{1,0:T(8,128)} %get-tuple-element.5) | copy-start | bytes 1572868
